TPU v7x, 32 devices: a whole 2x2x4 slice. The times are simulated.
32 devices in a mesh: dp: 8 (over y, x, core), stream: 4 (over z).
Axes of the slice: x: 2, y: 2, z: 4, core: 2. Of those that a mesh axis runs over, the one named last changes fastest.
Arguments:
- inputs: bfloat16 [32, 1024, 512], P(('dp', 'stream')), may hold values from -60 to 60
- lengths: int32 [32], P(('dp', 'stream')), may hold values from 256 to 1024, as said below
- cotangent: bfloat16 [32, 1024, 512], P(('dp', 'stream')), may hold values from -6 to 6
- gain_one: bfloat16 [512], replicated, may hold values from 0.5 to 1.5
- shift_one: bfloat16 [512], replicated, may hold values from -2.5 to 2.5
- expand_one: bfloat16 [512, 2048], replicated, may hold values from -0.25 to 0.25
- lift_one: bfloat16 [2048], replicated, may hold values from -2.5 to 2.5
- reduce_one: bfloat16 [2048, 512], replicated, may hold values from -0.25 to 0.25
- offset_one: bfloat16 [512], replicated, may hold values from -2.5 to 2.5
- attend_gain: bfloat16 [512], replicated, may hold values from 0.5 to 1.5
- attend_shift: bfloat16 [512], replicated, may hold values from -2.5 to 2.5
- query_proj: bfloat16 [512, 512], replicated, may hold values from -0.25 to 0.25
- query_bias: bfloat16 [512], replicated, may hold values from -2.5 to 2.5
- key_proj: bfloat16 [512, 512], replicated, may hold values from -0.25 to 0.25
- value_proj: bfloat16 [512, 512], replicated, may hold values from -0.25 to 0.25
- value_bias: bfloat16 [512], replicated, may hold values from -2.5 to 2.5
- output_proj: bfloat16 [512, 512], replicated, may hold values from -1 to 1
- output_bias: bfloat16 [512], replicated, may hold values from -2.5 to 2.5
- mixing_gain: bfloat16 [512], replicated, may hold values from 0.5 to 1.5
- mixing_shift: bfloat16 [512], replicated, may hold values from -2.5 to 2.5
- point_first: bfloat16 [512, 1024], replicated, may hold values from -0.25 to 0.25
- first_bias: bfloat16 [1024], replicated, may hold values from -2.5 to 2.5
- depth_kernel: bfloat16 [9, 512], replicated, may hold values from -2 to 2
- batch_gain: bfloat16 [512], replicated, may hold values from 0.5 to 1.5
- batch_shift: bfloat16 [512], replicated, may hold values from -2.5 to 2.5
- point_second: bfloat16 [512, 512], replicated, may hold values from -0.375 to 0.375
- second_bias: bfloat16 [512], replicated, may hold values from -2.5 to 2.5
- gain_two: bfloat16 [512], replicated, may hold values from 0.5 to 1.5
- shift_two: bfloat16 [512], replicated, may hold values from -2.5 to 2.5
- expand_two: bfloat16 [512, 2048], replicated, may hold values from -0.25 to 0.25
- lift_two: bfloat16 [2048], replicated, may hold values from -2.5 to 2.5
- reduce_two: bfloat16 [2048, 512], replicated, may hold values from -0.25 to 0.25
- offset_two: bfloat16 [512], replicated, may hold values from -2.5 to 2.5
- final_gain: bfloat16 [512], replicated, may hold values from 0.5 to 1.5
- final_shift: bfloat16 [512], replicated, may hold values from -2.5 to 2.5
Outputs:
- block_output: bfloat16 [32, 1024, 512], P(('dp', 'stream'))
- input_gradient: bfloat16 [32, 1024, 512], P(('dp', 'stream'))
- gain_one_gradient: float32 [512], replicated
- shift_one_gradient: float32 [512], replicated
- expand_one_gradient: float32 [512, 2048], replicated
- lift_one_gradient: float32 [2048], replicated
- reduce_one_gradient: float32 [2048, 512], replicated
- offset_one_gradient: float32 [512], replicated
- attend_gain_gradient: float32 [512], replicated
- attend_shift_gradient: float32 [512], replicated
- query_proj_gradient: float32 [512, 512], replicated
- query_bias_gradient: float32 [512], replicated
- key_proj_gradient: float32 [512, 512], replicated
- value_proj_gradient: float32 [512, 512], replicated
- value_bias_gradient: float32 [512], replicated
- output_proj_gradient: float32 [512, 512], replicated
- output_bias_gradient: float32 [512], replicated
- mixing_gain_gradient: float32 [512], replicated
- mixing_shift_gradient: float32 [512], replicated
- point_first_gradient: float32 [512, 1024], replicated
- first_bias_gradient: float32 [1024], replicated
- depth_kernel_gradient: float32 [9, 512], replicated
- batch_gain_gradient: float32 [512], replicated
- batch_shift_gradient: float32 [512], replicated
- point_second_gradient: float32 [512, 512], replicated
- second_bias_gradient: float32 [512], replicated
- gain_two_gradient: float32 [512], replicated
- shift_two_gradient: float32 [512], replicated
- expand_two_gradient: float32 [512, 2048], replicated
- lift_two_gradient: float32 [2048], replicated
- reduce_two_gradient: float32 [2048, 512], replicated
- offset_two_gradient: float32 [512], replicated
- final_gain_gradient: float32 [512], replicated
- final_shift_gradient: float32 [512], replicated
- rms_stats: float32 [8], replicated
Inputs may be any that keep to these rules, and one draw needn't show every extreme that they name: `lengths`: one utterance has exactly 1024 valid frames and another exactly a quarter of 1024.
All inputs are finite; a program needn't handle non-finite values.
Results may differ from a plain program's by a relative error of at most 0.028.
Values sent between devices are 32-bit elements; how exact they have to be, the bound alone decides.
No kernel may reach another device: no remote copies, remote signals or barrier semaphores. Data moves between devices by JAX's collectives and lax.ppermute only.
A program may use at most 192 MiB of HBM per device.

v0:
```python
import jax
import jax.numpy as jnp
from jax import lax
from jax.sharding import PartitionSpec as P

HEADS = 8
HEAD = 64


EPSILON = 1e-05


def product(operand_one, operand_two):
    return jnp.dot(operand_one, operand_two, preferred_element_type=jnp.float32)


def row_contract(operand_one, operand_two):
    return lax.dot_general(
        operand_one, operand_two, (((0,), (0,)), ((), ())), preferred_element_type=jnp.float32
    )


def transposed_product(operand_one, operand_two):
    return lax.dot_general(
        operand_one, operand_two, (((1,), (1,)), ((), ())), preferred_element_type=jnp.float32
    )


def column_sum(values):
    return jnp.sum(values, axis=0, dtype=jnp.float32)


def flatten_all(pieces):
    return jnp.concatenate([piece.reshape(-1) for piece in pieces])


def split_flat(flat, pieces):
    result = []
    start = 0
    for piece in pieces:
        count = piece.size
        result.append(flat[start : start + count].reshape(piece.shape))
        start = start + count
    return result


def layer_norm(values, norm_gain, norm_shift):
    centre = jnp.mean(values, axis=-1, keepdims=True)
    centred = values - centre
    spread = jnp.mean(centred * centred, axis=-1, keepdims=True)
    return centred * lax.rsqrt(spread + EPSILON) * norm_gain + norm_shift


def silu_slope(inner_act):
    logistic = jax.nn.sigmoid(inner_act)
    return logistic * (1.0 + inner_act * (1.0 - logistic))


def depthwise(shaped, kernel):
    half_width = kernel.shape[0] // 2
    frames = shaped.shape[1]
    padded = jnp.pad(shaped, ((0, 0), (half_width, half_width), (0, 0)))
    summed = padded[:, 0:frames, :] * kernel[0]
    for tap_index in range(1, kernel.shape[0]):
        summed = summed + padded[:, tap_index : tap_index + frames, :] * kernel[tap_index]
    return summed


def gate_convolve(both_halves, kernel, validity_rows, utterances):
    half_cols = both_halves.shape[1] // 2
    gated_rows = (
        both_halves[:, :half_cols] * jax.nn.sigmoid(both_halves[:, half_cols:]) * validity_rows
    )
    shaped = gated_rows.reshape(utterances, -1, half_cols)
    return depthwise(shaped, kernel).reshape(-1, half_cols)


def norm_forward(stream, norm_gain, norm_shift):
    return jax.vjp(
        layer_norm, stream, norm_gain.astype(jnp.float32), norm_shift.astype(jnp.float32)
    )


def feed_forward(stream, params):
    norm_gain, norm_shift, expand, lift_bias, reducer, offset = params
    normed, norm_back = norm_forward(stream, norm_gain, norm_shift)
    normed_low = normed.astype(jnp.bfloat16)
    inner_act = product(normed_low, expand) + lift_bias.astype(jnp.float32)
    activated = jax.nn.silu(inner_act).astype(jnp.bfloat16)
    branch = 0.5 * (product(activated, reducer) + offset.astype(jnp.float32))
    return (branch, (norm_back, normed_low, inner_act, activated))


def feed_backward(grad_stream, params, stored):
    norm_gain, norm_shift, expand, lift_bias, reducer, offset = params
    norm_back, normed_low, inner_act, activated = stored
    branch_low = (0.5 * grad_stream).astype(jnp.bfloat16)
    grad_reducer = row_contract(activated, branch_low)
    grad_offset = column_sum(branch_low)
    grad_activated = transposed_product(branch_low, reducer)
    inner_low = (grad_activated * silu_slope(inner_act)).astype(jnp.bfloat16)
    grad_expand = row_contract(normed_low, inner_low)
    grad_lift = column_sum(inner_low)
    grad_input, grad_gain, grad_shift = norm_back(transposed_product(inner_low, expand))
    return (
        grad_stream + grad_input,
        [grad_gain, grad_shift, grad_expand, grad_lift, grad_reducer, grad_offset],
    )


def masked_scores(query_block, keys_here, mask_here):
    scores = jnp.einsum(
        "qhd,khd->hqk", query_block, keys_here, preferred_element_type=jnp.float32
    ) * HEAD ** (-0.5)
    return jnp.where(mask_here[None, None, :], scores, -1e30)


def attend_forward(stream, params, key_mask):
    (
        norm_gain,
        norm_shift,
        query_proj,
        query_bias,
        key_proj,
        value_proj,
        value_bias,
        output_proj,
        output_bias,
    ) = params
    utterances, frames = key_mask.shape
    normed, norm_back = norm_forward(stream, norm_gain, norm_shift)
    normed_low = normed.astype(jnp.bfloat16)
    layout = (utterances, frames, HEADS, HEAD)
    queries = (
        (product(normed_low, query_proj) + query_bias.astype(jnp.float32))
        .astype(jnp.bfloat16)
        .reshape(layout)
    )
    key_rows = product(normed_low, key_proj).astype(jnp.bfloat16).reshape(layout)
    value_rows = (
        (product(normed_low, value_proj) + value_bias.astype(jnp.float32))
        .astype(jnp.bfloat16)
        .reshape(layout)
    )
    block_rows = min(512, frames)
    block_count = frames // block_rows
    keys_here = key_rows[0]
    values_here = value_rows[0]
    mask_here = key_mask[0]

    def forward_block(carried, query_block):
        scores = masked_scores(query_block, keys_here, mask_here)
        row_top = jnp.max(scores, axis=-1, keepdims=True)
        raised = jnp.exp(scores - row_top)
        totals = jnp.sum(raised, axis=-1, keepdims=True)
        softened = (raised / totals).astype(jnp.bfloat16)
        mixture = jnp.einsum(
            "hqk,khd->qhd", softened, values_here, preferred_element_type=jnp.float32
        )
        return (carried, (mixture.astype(jnp.bfloat16), row_top + jnp.log(totals)))

    unused, (mixture, log_total) = lax.scan(
        forward_block, 0, queries[0].reshape(block_count, block_rows, HEADS, HEAD)
    )
    mixtures = mixture.reshape(frames, HEADS * HEAD)
    log_totals = [log_total]
    branch = product(mixtures, output_proj) + output_bias.astype(jnp.float32)
    return (branch, (norm_back, normed_low, queries, key_rows, value_rows, mixtures, log_totals))


def attend_backward(grad_stream, params, stored, key_mask):
    (
        norm_gain,
        norm_shift,
        query_proj,
        query_bias,
        key_proj,
        value_proj,
        value_bias,
        output_proj,
        output_bias,
    ) = params
    norm_back, normed_low, queries, key_rows, value_rows, mixed, log_totals = stored
    utterances, frames = key_mask.shape
    block_rows = min(512, frames)
    block_count = frames // block_rows
    out_low = grad_stream.astype(jnp.bfloat16)
    grad_output = row_contract(mixed, out_low)
    grad_output_bias = column_sum(out_low)
    grad_mixed = (
        transposed_product(out_low, output_proj)
        .astype(jnp.bfloat16)
        .reshape(utterances, frames, HEADS, HEAD)
    )
    keys_here = key_rows[0]
    values_here = value_rows[0]
    mask_here = key_mask[0]

    def backward_block(carried, pieces):
        keys_total, values_total = carried
        query_block, mixed_block, log_block = pieces
        softened = jnp.exp(masked_scores(query_block, keys_here, mask_here) - log_block)
        soft_low = softened.astype(jnp.bfloat16)
        values_total = values_total + jnp.einsum(
            "hqk,qhd->khd", soft_low, mixed_block, preferred_element_type=jnp.float32
        )
        grad_soft = jnp.einsum(
            "qhd,khd->hqk", mixed_block, values_here, preferred_element_type=jnp.float32
        )
        inner_sum = jnp.sum(softened * grad_soft, axis=-1, keepdims=True)
        score_low = (softened * (grad_soft - inner_sum)).astype(jnp.bfloat16)
        query_grad = (
            jnp.einsum("hqk,khd->qhd", score_low, keys_here, preferred_element_type=jnp.float32)
            * HEAD ** (-0.5)
        ).astype(jnp.bfloat16)
        keys_total = keys_total + jnp.einsum(
            "hqk,qhd->khd", score_low, query_block, preferred_element_type=jnp.float32
        ) * HEAD ** (-0.5)
        return ((keys_total, values_total), query_grad)

    zeros_here = jnp.zeros((frames, HEADS, HEAD), jnp.float32)
    (keys_total, values_total), query_grad = lax.scan(
        backward_block,
        (zeros_here, zeros_here),
        (
            queries[0].reshape(block_count, block_rows, HEADS, HEAD),
            grad_mixed[0].reshape(block_count, block_rows, HEADS, HEAD),
            log_totals[0],
        ),
    )
    query_grads = query_grad.reshape(frames, HEADS * HEAD)
    key_grads = keys_total.astype(jnp.bfloat16).reshape(frames, HEADS * HEAD)
    value_grads = values_total.astype(jnp.bfloat16).reshape(frames, HEADS * HEAD)
    grad_normed = transposed_product(query_grads, query_proj) + transposed_product(
        key_grads, key_proj
    )
    grad_normed = grad_normed + transposed_product(value_grads, value_proj)
    grad_input, grad_gain, grad_shift = norm_back(grad_normed)
    return (
        grad_stream + grad_input,
        [
            grad_gain,
            grad_shift,
            row_contract(normed_low, query_grads),
            column_sum(query_grads),
            row_contract(normed_low, key_grads),
            row_contract(normed_low, value_grads),
            column_sum(value_grads),
            grad_output,
            grad_output_bias,
        ],
    )


def mixing_front(stream, params, validity_rows, utterances):
    norm_gain, norm_shift, point_first, first_bias, depth_kernel = params[0:5]
    normed, norm_back = norm_forward(stream, norm_gain, norm_shift)
    normed_low = normed.astype(jnp.bfloat16)
    doubled = product(normed_low, point_first) + first_bias.astype(jnp.float32)
    convolved, front_back = jax.vjp(
        lambda both_halves, kernel: gate_convolve(both_halves, kernel, validity_rows, utterances),
        doubled,
        depth_kernel.astype(jnp.float32),
    )
    return (convolved, (norm_back, normed_low, front_back))


def mixing_rear(convolved, batch_mean, inverse_std, params):
    batch_gain, batch_shift, point_second, second_bias = params[5:9]
    centred = convolved - batch_mean
    normal_out = centred * inverse_std * batch_gain.astype(jnp.float32) + batch_shift.astype(
        jnp.float32
    )
    activated = jax.nn.silu(normal_out).astype(jnp.bfloat16)
    branch = product(activated, point_second) + second_bias.astype(jnp.float32)
    return (branch, (centred, normal_out, activated))


def mixing_backward(
    grad_stream, params, front_stored, rear_stored, validity_rows, frame_count, inverse_std
):
    point_first = params[2]
    batch_gain = params[5]
    point_second = params[7]
    norm_back, normed_low, front_back = front_stored
    centred, normal_out, activated = rear_stored
    low_grad = grad_stream.astype(jnp.bfloat16)
    grad_point_second = row_contract(activated, low_grad)
    grad_second_bias = column_sum(low_grad)
    grad_normal = transposed_product(low_grad, point_second) * silu_slope(normal_out)
    grad_batch_gain = column_sum(grad_normal * centred * inverse_std)
    grad_batch_shift = column_sum(grad_normal)
    direct = grad_normal * batch_gain.astype(jnp.float32) * inverse_std
    mean_total, spread_total = lax.psum(
        (-column_sum(direct), -0.5 * inverse_std * inverse_std * column_sum(direct * centred)),
        ("dp", "stream"),
    )
    grad_convolved = (
        direct + validity_rows * (mean_total + 2.0 * spread_total * centred) / frame_count
    )
    grad_doubled, grad_kernel = front_back(grad_convolved)
    doubled_low = grad_doubled.astype(jnp.bfloat16)
    grad_point_first = row_contract(normed_low, doubled_low)
    grad_first_bias = column_sum(doubled_low)
    grad_input, grad_gain, grad_shift = norm_back(transposed_product(doubled_low, point_first))
    return (
        grad_stream + grad_input,
        [
            grad_gain,
            grad_shift,
            grad_point_first,
            grad_first_bias,
            grad_kernel,
            grad_batch_gain,
            grad_batch_shift,
            grad_point_second,
            grad_second_bias,
        ],
    )


def body(
    inputs,
    lengths,
    cotangent,
    gain_one,
    shift_one,
    expand_one,
    lift_one,
    reduce_one,
    offset_one,
    attend_gain,
    attend_shift,
    query_proj,
    query_bias,
    key_proj,
    value_proj,
    value_bias,
    output_proj,
    output_bias,
    mixing_gain,
    mixing_shift,
    point_first,
    first_bias,
    depth_kernel,
    batch_gain,
    batch_shift,
    point_second,
    second_bias,
    gain_two,
    shift_two,
    expand_two,
    lift_two,
    reduce_two,
    offset_two,
    final_gain,
    final_shift,
):
    first_block = [gain_one, shift_one, expand_one, lift_one, reduce_one, offset_one]
    attend_block = [
        attend_gain,
        attend_shift,
        query_proj,
        query_bias,
        key_proj,
        value_proj,
        value_bias,
        output_proj,
        output_bias,
    ]
    mixing_block = [
        mixing_gain,
        mixing_shift,
        point_first,
        first_bias,
        depth_kernel,
        batch_gain,
        batch_shift,
        point_second,
        second_bias,
    ]
    second_block = [gain_two, shift_two, expand_two, lift_two, reduce_two, offset_two]
    utterances, frames, model_width = inputs.shape
    key_mask = lax.broadcasted_iota(jnp.int32, (utterances, frames), 1) < lengths[:, None]
    validity_rows = key_mask.astype(jnp.float32).reshape(utterances * frames, 1)
    stream = inputs.astype(jnp.float32).reshape(-1, model_width)
    first_branch, first_stored = feed_forward(stream, first_block)
    after_first = stream + first_branch
    attend_branch, attend_stored = attend_forward(after_first, attend_block, key_mask)
    after_attend = after_first + attend_branch
    convolved, front_stored = mixing_front(after_attend, mixing_block, validity_rows, utterances)
    frames_here = jnp.sum(validity_rows)
    frame_count, summed = lax.psum(
        (frames_here, column_sum(convolved * validity_rows)), ("dp", "stream")
    )
    batch_mean = summed / frame_count
    centred_valid = (convolved - batch_mean) * validity_rows
    batch_var = lax.psum(column_sum(centred_valid * centred_valid), ("dp", "stream")) / frame_count
    inverse_std = lax.rsqrt(batch_var + EPSILON)
    mixing_branch, rear_stored = mixing_rear(convolved, batch_mean, inverse_std, mixing_block)
    after_mixing = after_attend + mixing_branch
    second_branch, second_stored = feed_forward(after_mixing, second_block)
    after_second = after_mixing + second_branch
    output, final_back = jax.vjp(
        lambda section, norm_gain, norm_shift: validity_rows
        * layer_norm(section, norm_gain, norm_shift),
        after_second,
        final_gain.astype(jnp.float32),
        final_shift.astype(jnp.float32),
    )
    squares = jnp.stack(
        [
            jnp.sum(validity_rows * section * section)
            for section in (
                after_first,
                after_attend,
                after_mixing,
                after_second,
                first_branch,
                attend_branch,
                mixing_branch,
                second_branch,
            )
        ]
    )
    grad_after, closing_gain, closing_shift = final_back(
        cotangent.astype(jnp.float32).reshape(-1, model_width)
    )
    grad_after, second_grads = feed_backward(grad_after, second_block, second_stored)
    grad_after, mixing_grads = mixing_backward(
        grad_after, mixing_block, front_stored, rear_stored, validity_rows, frame_count, inverse_std
    )
    late_pieces = second_grads + mixing_grads + [closing_gain, closing_shift, squares]
    grad_after, attend_grads = attend_backward(grad_after, attend_block, attend_stored, key_mask)
    grad_after, first_grads = feed_backward(grad_after, first_block, first_stored)
    early_pieces = first_grads + attend_grads
    every_flat = lax.psum(flatten_all(early_pieces + late_pieces), ("dp", "stream"))
    every_sum = split_flat(every_flat, early_pieces + late_pieces)
    early_sums = every_sum[0:15]
    late_sums = every_sum[15:]
    rms_stats = jnp.sqrt(late_sums[17] / (frame_count * model_width))
    block_output = output.reshape(utterances, frames, model_width).astype(jnp.bfloat16)
    input_gradient = grad_after.reshape(utterances, frames, model_width).astype(jnp.bfloat16)
    return (
        block_output,
        input_gradient,
        *early_sums[0:6],
        *early_sums[6:15],
        *late_sums[6:15],
        *late_sums[0:6],
        late_sums[15],
        late_sums[16],
        rms_stats,
    )


def solution(mesh):
    placed = (
        P(("dp", "stream"), None, None),
        P(("dp", "stream")),
        P(("dp", "stream"), None, None),
        P(),
        P(),
        P(),
        P(),
        P(),
        P(),
        P(),
        P(),
        P(),
        P(),
        P(),
        P(),
        P(),
        P(),
        P(),
        P(),
        P(),
        P(),
        P(),
        P(),
        P(),
        P(),
        P(),
        P(),
        P(),
        P(),
        P(),
        P(),
        P(),
        P(),
        P(),
        P(),
    )
    return jax.shard_map(
        body,
        mesh=mesh,
        in_specs=placed,
        out_specs=(
            P(("dp", "stream"), None, None),
            P(("dp", "stream"), None, None),
            P(),
            P(),
            P(),
            P(),
            P(),
            P(),
            P(),
            P(),
            P(),
            P(),
            P(),
            P(),
            P(),
            P(),
            P(),
            P(),
            P(),
            P(),
            P(),
            P(),
            P(),
            P(),
            P(),
            P(),
            P(),
            P(),
            P(),
            P(),
            P(),
            P(),
            P(),
            P(),
            P(),
        ),
        check_vma=False,
    )
```

profile of v0, /device:TPU:0, one launch (start us, length us, event | category | flops | bytes accessed | tf_op | source)
XLA Modules:
  0.0 1131.1 jit_solution(8133752081412010741)
XLA Ops:
  36.5 7.8 multiply_convert_fusion.4
  44.3 3.8 fusion.114
  53.2 3.3 copy.114
  61.6 28.0 %while.28 = (s32[]{:T(128)}, bf16[2,512,8,64]{1,3,2,0:T(8,128)(2,1)}, f32[2,8,512,1]{2,1,3,0:T(8,128)S(1)}, bf16[2,512,8,64]{1,3,2,0:T(8,128)(2,1)}, bf16[1024,8...) while((s32[]{:T(128)}, bf16[2,512,8,64]{1,3,2,0:T(8,128)(2,1)}, ...), condition=%wide.region_7.8_spmd.clone, body=%wide.region_4.7_spmd.clone.sunk | while | flops 1124332544 | bytes 66195648 | solution.py:162
  62.4 3.6 fusion.200
  66.0 4.0 fusion.201
  70.0 4.7 fusion.202
  76.3 3.6 fusion.200
  79.9 4.0 fusion.201
  83.9 4.7 fusion.202
  98.8 7.2 fusion.54
  106.1 42.2 %all-reduce.22 = (f32[512]{0:T(512)S(1)}, f32[]{:T(128)}) all-reduce(f32[512]{0:T(512)S(1)} %get-tuple-element.377, f32[]{:T(128)} %fusion.86), channel_id=1, replica_groups=mesh['dp'=8,'stream'=4] {'dp','stream'}, use_global_device_ids=true, to_apply=%region_11.12 | all-reduce | flops 513 | bytes 4104 | tf_op jit(solution)/shard_map/psum | solution.py:393
  150.9 40.8 %psum.44 = f32[512]{0:T(512)S(1)} all-reduce(f32[512]{0:T(512)S(1)} %multiply_reduce_fusion.14), channel_id=1, replica_groups=mesh['dp'=8,'stream'=4] {'dp','stream'}, use_global_device_ids=true, to_apply=%region_15.16 | all-reduce | flops 512 | bytes 4096 | tf_op jit(solution)/shard_map/psum | solution.py:398
  197.9 4.0 multiply_convert_fusion.3
  201.9 3.6 multiply_reduce_fusion.1
  210.4 4.7 convolution_bitcast_fusion
  215.2 5.4 convert_reduce_fusion
  220.5 4.3 fusion.122
  224.8 4.5 convolution_bitcast_fusion.1
  229.3 3.1 copy.119
  232.4 3.2 fusion.52
  237.5 3.6 convert_reduce_fusion.4
  243.9 3.6 multiply_reduce_fusion.3
  248.2 40.4 %all-reduce.21 = (f32[512]{0:T(512)S(1)}, f32[512]{0:T(512)S(1)}) all-reduce(f32[512]{0:T(512)S(1)} %fusion.94, f32[512]{0:T(512)S(1)} %neg.41), channel_id=1, replica_groups=mesh['dp'=8,'stream'=4] {'dp','stream'}, use_global_device_ids=true, to_apply=%region_27.28 | all-reduce | flops 1024 | bytes 8192 | tf_op jit(solution)/shard_map/psum | solution.py:294
  288.6 4.9 multiply_reduce_fusion.4
  293.5 6.4 fusion.68
  303.5 3.7 fusion.49
  309.3 2.6 convolution_bitcast_fusion.4
  311.9 3.2 fusion.123
  315.2 3.0 copy.121
  318.2 3.4 multiply_reduce_fusion.5
  329.0 3.5 copy.124
  333.6 77.8 %while.29 = (s32[]{:T(128)}, f32[1024,8,64]{0,2,1:T(8,128)S(1)}, f32[1024,8,64]{0,2,1:T(8,128)}, bf16[2,512,8,64]{1,3,2,0:T(8,128)(2,1)}, bf16[2,512,8,64]{1,3,2...) while((s32[]{:T(128)}, f32[1024,8,64]{0,2,1:T(8,128)S(1)}, ...), condition=%wide.region_32.33_spmd.clone, body=%wide.region_30.32_spmd.clone.sunk | while | flops 2725245952 | bytes 198789488 | solution.py:222
  334.5 3.8 fusion.212
  338.3 10.4 multiply_reduce_fusion.18
  348.7 9.5 multiply_convert_fusion.13
  358.2 8.9 bitcast_add_fusion.6
  367.5 2.7 fusion.213
  373.0 3.8 fusion.212
  376.7 10.4 multiply_reduce_fusion.18
  387.1 9.5 multiply_convert_fusion.13
  396.7 9.5 bitcast_add_fusion.6
  406.5 2.7 fusion.213
  431.2 4.5 convolution_bitcast_fusion.2
  435.7 4.7 convert_reduce_fusion.1
  440.4 3.8 fusion.121
  444.3 4.5 convolution_bitcast_fusion.3
  448.8 3.2 copy.154
  452.0 2.9 copy.153
  455.8 3.4 copy.155
  459.6 2.6 copy.149
  463.5 2.5 copy.151
  465.9 5.5 copy.148
  471.4 2.9 copy.147
  474.3 2.9 copy.129
  480.6 209.0 %concatenate.3 = f32[6048264]{0:T(1024)} concatenate(f32[512]{0:T(512)S(1)} %get-tuple-element.359, f32[512]{0:T(512)S(1)} %get-tuple-element.506, f32[1048576]{0:T(1024)} %bitcast.343, f32[2048]{0:T(1024)S(1)} %get-tuple-element.508, f32[1048576]{0:T(1024)} %bitcast.342, f32[512]{0:T(512)S(1)} %get-tuple-element.426, f32[512]{0:T(512)S(1)} %get-tuple-element.343, ...), dimensions={0} | concatenate | bytes 48386112 | tf_op jit(solution)/shard_map/concatenate | solution.py:34
  692.1 2.9 fusion.83
  696.4 373.6 %all-reduce.25.cloned.1.call-done = f32[6048264]{0:T(1024)} async-done(((f32[6048264]{0:T(1024)}), f32[6048264]{0:T(1024)}) %all-reduce.25.cloned.1.call-update) | async-done | bytes 24193072 | tf_op jit(solution)/shard_map/psum | solution.py:437
  1074.5 12.2 %fusion.117 = (f32[1048576]{0:T(1024)}, f32[1048576]{0:T(1024)}, f32[1048576]{0:T(1024)}, f32[1048576]{0:T(1024)}) fusion(f32[6048264]{0:T(1024)} %all-reduce.25.cloned.1.call-done), kind=kLoop, calls=%fused_computation.267 | loop fusion | bytes 33554432 | tf_op jit(solution)/shard_map/slice | solution.py:42
  1086.7 4.9 reshape.524
  1091.7 4.1 fusion.119
  1103.9 4.9 reshape.523
  1108.8 4.9 reshape.515
  1113.7 5.0 reshape.514
  (454 shorter events, 136.6 us)
Async XLA Ops:
  7.2 190.2 %copy-start = (bf16[512,2048]{1,0:T(8,128)(2,1)S(1)}, bf16[512,2048]{1,0:T(8,128)(2,1)}, u32[]{:S(2)}) copy-start(bf16[512,2048]{1,0:T(8,128)(2,1)} %param.68) | copy-start | bytes 6291460
  7.2 1062.7 %all-reduce.25.cloned.1.call-start = ((), (), s32[]{:S(2)}) async-start(), calls=%async_computation | async-start | bytes 48390144 | tf_op jit(solution)/shard_map/psum | solution.py:437
  9.4 27.0 %copy-start.84 = (f32[512]{0:T(512)}, f32[512]{0:T(512)S(1)}, u32[]{:S(2)}) copy-start(f32[512]{0:T(512)S(1)} %convert_element_type.212) | copy-start | bytes 6148
  11.4 37.1 %copy-start.73 = (f32[512]{0:T(512)}, f32[512]{0:T(512)S(1)}, u32[]{:S(2)}) copy-start(f32[512]{0:T(512)S(1)} %convert_element_type.218) | copy-start | bytes 6148
  15.8 20.7 %copy-start.129 = (f32[512]{0:T(512)}, f32[512]{0:T(512)S(1)}, u32[]{:S(2)}) copy-start(f32[512]{0:T(512)S(1)} %convert_element_type.213) | copy-start | bytes 6148
  16.5 27.8 %copy-start.133 = (f32[512]{0:T(512)}, f32[512]{0:T(512)S(1)}, u32[]{:S(2)}) copy-start(f32[512]{0:T(512)S(1)} %convert_element_type.217) | copy-start | bytes 6148
  29.2 7.2 copy-start.117
  33.6 10.7 copy-start.19
  33.8 10.4 copy-start.69
  34.2 10.1 copy-start.76
  34.2 10.1 copy-start.80
  36.5 7.8 copy-start.138
  44.3 3.8 copy-start.143
  66.0 4.0 copy-start.8
  66.0 4.0 copy-start.47
  79.9 4.0 copy-start.8
  79.9 4.0 copy-start.47
  93.2 3.5 copy-start.15
  97.6 8.4 copy-start.32
  106.1 86.4 %copy-start.97 = (f32[512]{0:T(512)S(1)}, f32[512]{0:T(512)}, u32[]{:S(2)}) copy-start(f32[512]{0:T(512)} %convert_element_type.233) | copy-start | bytes 6148
  106.1 86.4 %copy-start.116 = (f32[512]{0:T(512)S(1)}, f32[512]{0:T(512)}, u32[]{:S(2)}) copy-start(f32[512]{0:T(512)} %convert_element_type.234) | copy-start | bytes 6148
  150.9 44.0 %copy-start.99 = (f32[512]{0:T(512)S(1)}, f32[512]{0:T(512)}, u32[]{:S(2)}) copy-start(f32[512]{0:T(512)} %convert_element_type.236) | copy-start | bytes 6148
  191.7 3.2 copy-start.16
  191.7 3.2 copy-start.58
  197.0 27.8 %copy-start.13 = (f32[1024,512]{0,1:T(8,128)}, f32[1024,512]{0,1:T(8,128)S(1)}, u32[]{:S(2)}) copy-start(f32[1024,512]{0,1:T(8,128)S(1)} %get-tuple-element.435) | copy-start | bytes 6291460
  197.8 4.0 copy-start.123
  197.8 4.0 copy-start.134
  197.8 4.0 copy-start.135
  197.8 4.0 copy-start.137
  197.8 4.0 copy-start.145
  201.9 3.6 copy-start.29
  201.9 3.6 copy-start.75
  205.5 3.4 copy-start.23
  224.8 4.5 copy-start.136
  232.4 3.2 copy-start.25
  237.5 3.6 copy-start.37
  288.6 4.9 copy-start.33
  318.2 3.4 copy-start.31
  329.0 4.5 copy-start.3
  348.7 9.5 copy-start.18
  358.2 8.9 copy-start.2
  358.2 8.9 copy-start.5
  358.2 9.2 copy-start.38
  387.1 9.5 copy-start.18
  396.6 9.5 copy-start.2
  396.6 9.5 copy-start.5
  396.6 9.8 copy-start.38
  420.7 3.7 copy-start.41
  428.9 6.8 slice-start
  430.1 5.6 copy-start.40
  431.2 4.5 copy-start.118
  431.2 4.5 copy-start.139
  431.2 4.5 slice-start.1
  435.7 4.7 copy-start.140
  440.4 3.9 copy-start.20
  440.4 3.9 copy-start.70
  440.4 3.9 copy-start.81
  440.4 3.9 copy-start.85
  440.4 3.9 copy-start.130
  444.3 4.5 copy-start.44
  448.8 3.2 copy-start.45
  455.8 3.5 copy-start.54
  465.9 5.5 copy-start.46
  1113.7 10.3 copy-start.1
  (95 other events, 155.8 us)
Sparse Core Ops, SparseCore 0:
  689.7 380.1 all-reduce.24
where the time goes:
time: 1150 us; the launch traced here: 1130 us
  waiting for transfers between devices  374 us (33%)
  local copies, waits for them, and re-layouts  338 us (29%)
  matrix products  159 us (14%)
  blocking collectives  123 us (11%)
  other arithmetic  119 us (10%)
  between operations  17.3 us (2%)
    psum x1, waiting for transfers between devices, body(): lax.psum(flatten_all(early_pieces + late_pieces), ('dp', 'stream'))  374 us
    concatenate x1, local copies, waits for them, and re-layouts, flatten_all(): return jnp.concatenate([piece.reshape(-1) for piece in pieces])  209 us
    unnamed x294, local copies, waits for them, and re-layouts  51.1 us
    psum x1, blocking collectives, body(): lax.psum((frames_here, column_sum(convolved * validity_rows)), ('dp', 'st...  42.2 us
    psum x1, blocking collectives, body(): lax.psum(column_sum(centred_valid * centred_valid), ('dp', 'stream'))  40.8 us
    psum x1, blocking collectives, mixing_backward(): lax.psum((-column_sum(direct), -0.5 * inverse_std * inverse_std * column_...  40.4 us
    reshape x11, local copies, waits for them, and re-layouts, split_flat(): result.append(flat[start:start + count].reshape(piece.shape))  29.9 us
    dot_general x10, matrix products, row_contract(): lax.dot_general(operand_one, operand_two, (((0,), (0,)), ((), ())), prefe...  29.5 us
  transfers between devices with their start and end apart: 1, of which 1 were waited for; matrix products, arithmetic and copies ran while one was open for 0% of the time, Pallas kernels for 0%

commit v1 on v0

--- a/solution.py
+++ b/solution.py
@@ -30,18 +30,79 @@
     return jnp.sum(values, axis=0, dtype=jnp.float32)
 
 
-def flatten_all(pieces):
-    return jnp.concatenate([piece.reshape(-1) for piece in pieces])
-
-
-def split_flat(flat, pieces):
-    result = []
-    start = 0
-    for piece in pieces:
-        count = piece.size
-        result.append(flat[start : start + count].reshape(piece.shape))
-        start = start + count
-    return result
+AXES = ("dp", "stream")
+
+
+def bits_of(axis):
+    return lax.axis_size(axis).bit_length() - 1
+
+
+def exchange(values, axis, bit):
+    count = lax.axis_size(axis)
+    return lax.ppermute(values, axis, [(at, at ^ (1 << bit)) for at in range(count)])
+
+
+def own_bit(axis, bit):
+    return (lax.axis_index(axis) >> bit) & 1
+
+
+def every_bit():
+    return [(axis, bit) for axis in AXES for bit in range(bits_of(axis))]
+
+
+def halve(values, axis, bit):
+    half = values.shape[0] // 2
+    mine = own_bit(axis, bit)
+    arrived = exchange(
+        lax.dynamic_slice_in_dim(values, (1 - mine) * half, half), axis, bit
+    )
+    return lax.dynamic_slice_in_dim(values, mine * half, half) + arrived
+
+
+def double(values, axis, bit):
+    arrived = exchange(values, axis, bit)
+    upper = own_bit(axis, bit) == 1
+    return jnp.concatenate(
+        [jnp.where(upper, arrived, values), jnp.where(upper, values, arrived)]
+    )
+
+
+def sum_parts(parts):
+    pair = every_bit()[0]
+    rest_dp = [step for step in every_bit()[1:] if step[0] == "dp"]
+    rest_stream = [step for step in every_bit() if step[0] == "stream"]
+    orders = [
+        [pair] + rest_dp + rest_stream,
+        [pair] + rest_dp[::-1] + rest_stream,
+        [pair] + rest_stream + rest_dp,
+    ]
+    steps = len(orders[0])
+    for at in range(steps):
+        parts = [halve(part, *orders[which % 3][at]) for which, part in enumerate(parts)]
+    for at in reversed(range(steps)):
+        parts = [double(part, *orders[which % 3][at]) for which, part in enumerate(parts)]
+    return parts
+
+
+def sum_small(values):
+    for axis, bit in every_bit():
+        values = values + exchange(values, axis, bit)
+    return values
+
+
+def batch_moments(convolved, validity_rows):
+    count = jnp.sum(validity_rows)
+    summed = column_sum(convolved * validity_rows)
+    apart = (convolved - summed / count) * validity_rows
+    spread = column_sum(apart * apart)
+    packed = jnp.stack([jnp.full_like(summed, count), summed, spread])
+    for axis, bit in every_bit():
+        other = exchange(packed, axis, bit)
+        both = packed + other
+        gap = packed[1] / packed[0] - other[1] / other[0]
+        extra = gap * gap * (packed[0] * other[0] / both[0])
+        packed = jnp.stack([both[0], both[1], both[2] + extra])
+    return packed[0, 0], packed[1] / packed[0], packed[2] / packed[0]
 
 
 def layer_norm(values, norm_gain, norm_shift):
@@ -291,9 +352,10 @@
     grad_batch_gain = column_sum(grad_normal * centred * inverse_std)
     grad_batch_shift = column_sum(grad_normal)
     direct = grad_normal * batch_gain.astype(jnp.float32) * inverse_std
-    mean_total, spread_total = lax.psum(
-        (-column_sum(direct), -0.5 * inverse_std * inverse_std * column_sum(direct * centred)),
-        ("dp", "stream"),
+    mean_total, spread_total = sum_small(
+        jnp.stack(
+            [-column_sum(direct), -0.5 * inverse_std * inverse_std * column_sum(direct * centred)]
+        )
     )
     grad_convolved = (
         direct + validity_rows * (mean_total + 2.0 * spread_total * centred) / frame_count
@@ -389,13 +451,7 @@
     attend_branch, attend_stored = attend_forward(after_first, attend_block, key_mask)
     after_attend = after_first + attend_branch
     convolved, front_stored = mixing_front(after_attend, mixing_block, validity_rows, utterances)
-    frames_here = jnp.sum(validity_rows)
-    frame_count, summed = lax.psum(
-        (frames_here, column_sum(convolved * validity_rows)), ("dp", "stream")
-    )
-    batch_mean = summed / frame_count
-    centred_valid = (convolved - batch_mean) * validity_rows
-    batch_var = lax.psum(column_sum(centred_valid * centred_valid), ("dp", "stream")) / frame_count
+    frame_count, batch_mean, batch_var = batch_moments(convolved, validity_rows)
     inverse_std = lax.rsqrt(batch_var + EPSILON)
     mixing_branch, rear_stored = mixing_rear(convolved, batch_mean, inverse_std, mixing_block)
     after_mixing = after_attend + mixing_branch
@@ -427,29 +483,98 @@
         cotangent.astype(jnp.float32).reshape(-1, model_width)
     )
     grad_after, second_grads = feed_backward(grad_after, second_block, second_stored)
+    second_large = lax.psum((second_grads[2], second_grads[4]), AXES)
     grad_after, mixing_grads = mixing_backward(
         grad_after, mixing_block, front_stored, rear_stored, validity_rows, frame_count, inverse_std
     )
-    late_pieces = second_grads + mixing_grads + [closing_gain, closing_shift, squares]
     grad_after, attend_grads = attend_backward(grad_after, attend_block, attend_stored, key_mask)
+    width = model_width
+    rows = []
+    for piece in (
+        second_grads[0],
+        second_grads[1],
+        second_grads[3],
+        second_grads[5],
+        *mixing_grads[0:2],
+        *mixing_grads[3:7],
+        mixing_grads[8],
+        closing_gain,
+        closing_shift,
+        *attend_grads[0:2],
+        attend_grads[3],
+        attend_grads[6],
+        attend_grads[8],
+        jnp.pad(squares, (0, width - 8)),
+    ):
+        rows.append(piece.reshape(-1, width))
+    small = jnp.concatenate(rows)
+    small_rows = small.shape[0]
+    small = jnp.pad(small, ((0, 128 - small_rows), (0, 0)))
+    large = jnp.concatenate(
+        [
+            mixing_grads[2][:, :width],
+            mixing_grads[2][:, width:],
+            mixing_grads[7],
+            attend_grads[2],
+            attend_grads[4],
+            attend_grads[5],
+            attend_grads[7],
+            small,
+        ]
+    )
+    cut = 1408
+    middle = jnp.concatenate(sum_parts([large[:cut], large[cut : 2 * cut], large[2 * cut :]]))
     grad_after, first_grads = feed_backward(grad_after, first_block, first_stored)
-    early_pieces = first_grads + attend_grads
-    every_flat = lax.psum(flatten_all(early_pieces + late_pieces), ("dp", "stream"))
-    every_sum = split_flat(every_flat, early_pieces + late_pieces)
-    early_sums = every_sum[0:15]
-    late_sums = every_sum[15:]
-    rms_stats = jnp.sqrt(late_sums[17] / (frame_count * model_width))
+    first_reduce, first_expand = sum_parts([first_grads[4], first_grads[2]])
+    first_small = sum_small(
+        jnp.concatenate(
+            [
+                first_grads[0][None],
+                first_grads[1][None],
+                first_grads[3].reshape(-1, width),
+                first_grads[5][None],
+            ]
+        )
+    )
+    squares = middle[7 * width + small_rows - 1, 0:8]
+    at = [7 * width]
+
+    def take(count):
+        piece = middle[at[0] : at[0] + count].reshape(-1)
+        at[0] = at[0] + count
+        return piece
+
+    second_sums = [take(1), take(1), second_large[0], take(4), second_large[1], take(1)]
+    mixing_sums = [take(1), take(1), None, take(2)]
+    mixing_sums = mixing_sums + [
+        middle[at[0] : at[0] + 9],
+    ]
+    at[0] = at[0] + 9
+    mixing_sums = mixing_sums + [take(1), take(1), middle[2 * width : 3 * width], take(1)]
+    mixing_sums[2] = jnp.concatenate([middle[:width], middle[width : 2 * width]], axis=1)
+    closing_sums = [take(1), take(1)]
+    attend_sums = [take(1), take(1), None, take(1), None, None, take(1), None, take(1)]
+    for slot, block in ((2, 3), (4, 4), (5, 5), (7, 6)):
+        attend_sums[slot] = middle[block * width : (block + 1) * width]
+    first_sums = [
+        first_small[0],
+        first_small[1],
+        first_expand,
+        first_small[2:-1].reshape(-1),
+        first_reduce,
+        first_small[-1],
+    ]
+    rms_stats = jnp.sqrt(squares / (frame_count * model_width))
     block_output = output.reshape(utterances, frames, model_width).astype(jnp.bfloat16)
     input_gradient = grad_after.reshape(utterances, frames, model_width).astype(jnp.bfloat16)
     return (
         block_output,
         input_gradient,
-        *early_sums[0:6],
-        *early_sums[6:15],
-        *late_sums[6:15],
-        *late_sums[0:6],
-        late_sums[15],
-        late_sums[16],
+        *first_sums,
+        *attend_sums,
+        *mixing_sums,
+        *second_sums,
+        *closing_sums,
         rms_stats,
     )
 

time: 1150 us -> 657 us (0.57)
  local copies, waits for them, and re-layouts: 338 us -> 88.9 us
  waiting for transfers between devices: 374 us -> 190 us
  blocking collectives: 123 us -> 0 us
  starting transfers between devices: 0.04 us -> 58.5 us
    psum x1, waiting for transfers between devices: 374 us -> 0.01 us  [body(): second_large = lax.psum((second_grads[2], second_grads[4]), AXES)]
    concatenate x1, local copies, waits for them, and re-layouts: 209 us -> 0.24 us  [body(): small = jnp.concatenate(rows)]
    ppermute x0 -> x65, waiting for transfers between devices: none -> 190 us  [exchange(): lax.ppermute(values, axis, [(at, at ^ 1 << bit) for at in range(count)])]
    psum x3 -> x0, blocking collectives: 123 us -> none  [the longest x1 42.2 us: body(): lax.psum((frames_here, column_sum(convolved * validity_rows)), ('dp', 'st...]
    ppermute x0 -> x65, starting transfers between devices: none -> 58.5 us  [exchange(): lax.ppermute(values, axis, [(at, at ^ 1 << bit) for at in range(count)])]
    reshape x12 -> x5, local copies, waits for them, and re-layouts: 29.9 us -> 0.77 us  [the longest x4 0.77 us: body(): rows.append(piece.reshape(-1, width))]
    slice x7 -> x10, local copies, waits for them, and re-layouts: 22.9 us -> 5.57 us  [the longest x1 3.13 us: body(): mixing_grads[2][:, :width]]
    concatenate x0 -> x27, other arithmetic: none -> 12.1 us  [the longest x22 6.15 us: double(): jnp.concatenate([jnp.where(upper, arrived, values), jnp.where(upper, valu...]
  transfers between devices with their start and end apart: 1 -> 66, of which waited for: 1 -> 39; matrix products, arithmetic and copies ran while one was open for 0% -> 36% of each run, Pallas kernels for 0% -> 0%
where the time goes in v1:
time: 657 us; the launch traced here: 649 us
  waiting for transfers between devices  190 us (29%)
  matrix products  162 us (25%)
  other arithmetic  129 us (20%)
  local copies, waits for them, and re-layouts  88.9 us (14%)
  starting transfers between devices  58.5 us (9%)
  between operations  18.5 us (3%)
    ppermute x65, waiting for transfers between devices, exchange(): lax.ppermute(values, axis, [(at, at ^ 1 << bit) for at in range(count)])  190 us
    ppermute x65, starting transfers between devices, exchange(): lax.ppermute(values, axis, [(at, at ^ 1 << bit) for at in range(count)])  58.5 us
    unnamed x322, local copies, waits for them, and re-layouts  42 us
    dot_general x10, matrix products, row_contract(): lax.dot_general(operand_one, operand_two, (((0,), (0,)), ((), ())), prefe...  33 us
    dot_general x10, matrix products, transposed_product(): lax.dot_general(operand_one, operand_two, (((1,), (1,)), ((), ())), prefe...  30.1 us
    dot_general x4, matrix products, masked_scores(): jnp.einsum('qhd,khd->hqk', query_block, keys_here, preferred_element_type...  28 us
    dot_general x10, matrix products, product(): return jnp.dot(operand_one, operand_two, preferred_element_type=jnp.float32)  26.4 us
    convert_element_type x2, other arithmetic, backward_block(): score_low = (softened * (grad_soft - inner_sum)).astype(jnp.bfloat16)  19.6 us
  transfers between devices with their start and end apart: 66, of which 39 were waited for; matrix products, arithmetic and copies ran while one was open for 36% of the time, Pallas kernels for 0%

profile of v1, /device:TPU:0, one launch (start us, length us, event | category | flops | bytes accessed | tf_op | source)
XLA Modules:
  0.0 648.5 jit_solution(4591089128370430669)
XLA Ops:
  24.9 6.0 multiply_convert_fusion.4
  31.0 3.8 fusion.139
  39.9 3.3 copy.114
  48.2 28.0 %while.28 = (s32[]{:T(128)}, bf16[2,512,8,64]{1,3,2,0:T(8,128)(2,1)}, f32[2,8,512,1]{2,1,3,0:T(8,128)S(1)}, bf16[2,512,8,64]{1,3,2,0:T(8,128)(2,1)}, bf16[1024,8...) while((s32[]{:T(128)}, bf16[2,512,8,64]{1,3,2,0:T(8,128)(2,1)}, ...), condition=%wide.region_7.8_spmd.clone, body=%wide.region_4.7_spmd.clone.sunk | while | flops 1124332544 | bytes 66195648 | solution.py:223
  49.0 3.6 fusion.231
  52.6 4.0 fusion.232
  56.6 4.7 fusion.233
  62.9 3.6 fusion.231
  66.5 4.0 fusion.232
  70.5 4.7 fusion.233
  85.5 6.5 fusion.54
  108.7 3.1 collective-permute-start.4
  119.6 4.0 multiply_convert_fusion.3
  123.7 3.6 multiply_reduce_fusion.1
  132.2 5.1 convert_reduce_fusion
  137.4 4.3 fusion.147
  141.7 3.1 copy.119
  144.8 3.1 fusion.52
  149.8 3.6 convert_reduce_fusion.7
  153.4 3.8 multiply_reduce_fusion.4
  163.7 7.2 %fusion.127 = f32[512,2048]{1,0:T(8,128)} fusion(bf16[1024,2048]{1,0:T(8,128)(2,1)} %copy-done.157, f32[1024,512]{0,1:T(8,128)} %copy-done.12, f32[512]{0:T(512)S(1)} %convert_element_type.242, f32[512]{0:T(512)S(1)} %convert_element_type.241, f32[1024]{0:T(1024)S(1)} %fusion.97, f32[1024]{0:T(1024)S(1)} %broadcast_multiply_fusion.1), kind=kOutput, calls=%fused_computation.432 | convolution fusion | flops 2150105088 | bytes 10498048 | tf_op jit(solution)/shard_map/dot_general | solution.py:18
  172.6 4.5 fusion.153
  178.9 3.7 fusion.109
  186.7 6.1 multiply_reduce_fusion.5
  192.8 6.4 fusion.69
  202.8 3.9 fusion.49
  211.5 3.2 fusion.148
  217.7 4.1 multiply_reduce_fusion.6
  228.2 3.9 reshape.611
  232.1 3.3 copy.124
  236.5 79.5 %while.29 = (s32[]{:T(128)}, f32[1024,8,64]{0,2,1:T(8,128)S(1)}, f32[1024,8,64]{0,2,1:T(8,128)}, bf16[2,512,8,64]{1,3,2,0:T(8,128)(2,1)}, bf16[2,512,8,64]{1,3,2...) while((s32[]{:T(128)}, f32[1024,8,64]{0,2,1:T(8,128)S(1)}, ...), condition=%wide.region_27.28_spmd.clone, body=%wide.region_25.27_spmd.clone.sunk | while | flops 2725245952 | bytes 198789488 | solution.py:283
  237.9 4.1 fusion.243
  242.0 10.5 %multiply_reduce_fusion.17 = (f32[8,512]{1,0:T(8,128)S(1)}, f32[8,512,1024]{2,1,0:T(8,128)}) fusion(f32[8,512,1024]{2,1,0:T(8,128)S(1)} %fusion.243, f32[8,512]{1,0:T(8,128)S(1)} %dynamic-slice_bitcast_fusion.2, bf16[1024,8,64]{0,2,1:T(8,128)(2,1)} %copy-done.3, bf16[2,512,8,64]{1,3,2,0:T(8,128)(2,1)} %get-tuple-element.732, s32[]{:T(128)S(6)} %copy.166, ...), kind=kOutput, calls=%fused_computation.20.clone.1 | convolution fusion | flops 557838336 | bytes 35161092 | tf_op jit(solution)/shard_map/while/body/eval_jaxpr/qhd,khd->hqk/dot_general | solution.py:173
  252.4 9.7 %multiply_convert_fusion.13 = bf16[8,512,1024]{2,1,0:T(8,128)(2,1)} fusion(f32[8,512,1024]{2,1,0:T(8,128)} %get-tuple-element.678, f32[8,512,1024]{2,1,0:T(8,128)S(1)} %fusion.243, f32[8,512]{1,0:T(8,128)S(1)} %get-tuple-element.679), kind=kLoop, calls=%fused_computation.19.clone.1 | loop fusion | flops 12582912 | bytes 41959424 | tf_op jit(solution)/shard_map/while/body/eval_jaxpr/convert_element_type | solution.py:272
  262.1 8.9 %bitcast_add_fusion.6 = f32[1024,8,64]{0,2,1:T(8,128)} fusion(f32[1024,8,64]{0,2,1:T(8,128)} %get-tuple-element.718, f32[8,512,1024]{2,1,0:T(8,128)} %get-tuple-element.678, pred[]{:T(512)S(6)} %compare.30, bf16[2,512,8,64]{1,3,2,0:T(8,128)(2,1)S(1)} %copy-done.18, s32[]{:T(128)S(6)} %copy.166), kind=kOutput, calls=%fused_computation.24.clone.1 | convolution fusion | flops 542113792 | bytes 21495812 | tf_op jit(solution)/shard_map/while/body/eval_jaxpr/hqk,qhd->khd/dot_general | solution.py:265
  277.2 3.8 fusion.243
  281.0 10.5 %multiply_reduce_fusion.17 = (f32[8,512]{1,0:T(8,128)S(1)}, f32[8,512,1024]{2,1,0:T(8,128)}) fusion(f32[8,512,1024]{2,1,0:T(8,128)S(1)} %fusion.243, f32[8,512]{1,0:T(8,128)S(1)} %dynamic-slice_bitcast_fusion.2, bf16[1024,8,64]{0,2,1:T(8,128)(2,1)} %copy-done.3, bf16[2,512,8,64]{1,3,2,0:T(8,128)(2,1)} %get-tuple-element.732, s32[]{:T(128)S(6)} %copy.166, ...), kind=kOutput, calls=%fused_computation.20.clone.1 | convolution fusion | flops 557838336 | bytes 35161092 | tf_op jit(solution)/shard_map/while/body/eval_jaxpr/qhd,khd->hqk/dot_general | solution.py:173
  291.4 9.9 %multiply_convert_fusion.13 = bf16[8,512,1024]{2,1,0:T(8,128)(2,1)} fusion(f32[8,512,1024]{2,1,0:T(8,128)} %get-tuple-element.678, f32[8,512,1024]{2,1,0:T(8,128)S(1)} %fusion.243, f32[8,512]{1,0:T(8,128)S(1)} %get-tuple-element.679), kind=kLoop, calls=%fused_computation.19.clone.1 | loop fusion | flops 12582912 | bytes 41959424 | tf_op jit(solution)/shard_map/while/body/eval_jaxpr/convert_element_type | solution.py:272
  301.4 9.5 %bitcast_add_fusion.6 = f32[1024,8,64]{0,2,1:T(8,128)} fusion(f32[1024,8,64]{0,2,1:T(8,128)} %get-tuple-element.718, f32[8,512,1024]{2,1,0:T(8,128)} %get-tuple-element.678, pred[]{:T(512)S(6)} %compare.30, bf16[2,512,8,64]{1,3,2,0:T(8,128)(2,1)S(1)} %copy-done.18, s32[]{:T(128)S(6)} %copy.166), kind=kOutput, calls=%fused_computation.24.clone.1 | convolution fusion | flops 542113792 | bytes 21495812 | tf_op jit(solution)/shard_map/while/body/eval_jaxpr/hqk,qhd->khd/dot_general | solution.py:265
  336.0 4.5 fusion.121
  341.1 4.7 convert_reduce_fusion.1
  345.9 3.7 fusion.146
  349.6 4.5 fusion.122
  354.4 3.1 fusion.141
  357.7 4.9 stack.77
  379.1 3.0 collective-permute-done.11
  389.8 5.9 collective-permute-done.13
  404.1 11.1 %collective-permute-done.37 = f32[112,512]{1,0:T(8,128)S(1)} collective-permute-done((f32[112,512]{1,0:T(8,128)S(1)}, f32[112,512]{1,0:T(8,128)S(1)}, u32[]{:S(2)}, u32[]{:S(2)}) %collective-permute-start.37) | collective-permute-done | bytes 229408 | tf_op jit(solution)/shard_map/ppermute | solution.py:42
  429.2 12.3 %collective-permute-done.40 = f32[28,512]{1,0:T(8,128)S(1)} collective-permute-done((f32[28,512]{1,0:T(8,128)S(1)}, f32[28,512]{1,0:T(8,128)S(1)}, u32[]{:S(2)}, u32[]{:S(2)}) %collective-permute-start.40) | collective-permute-done | bytes 57376 | tf_op jit(solution)/shard_map/ppermute | solution.py:42
  443.7 3.9 collective-permute-done.41
  452.9 10.2 %collective-permute-done.56 = f32[352,512]{1,0:T(8,128)S(1)} collective-permute-done((f32[352,512]{1,0:T(8,128)S(1)}, f32[352,512]{1,0:T(8,128)S(1)}, u32[]{:S(2)}, u32[]{:S(2)}) %collective-permute-start.56) | collective-permute-done | bytes 720928 | tf_op jit(solution)/shard_map/ppermute | solution.py:42
  464.4 26.6 %collective-permute-done.47 = f32[176,512]{1,0:T(8,128)S(1)} collective-permute-done((f32[176,512]{1,0:T(8,128)S(1)}, f32[176,512]{1,0:T(8,128)S(1)}, u32[]{:S(2)}, u32[]{:S(2)}) %collective-permute-start.47) | collective-permute-done | bytes 360480 | tf_op jit(solution)/shard_map/ppermute | solution.py:42
  493.3 4.4 collective-permute-done.48
  500.9 7.6 %collective-permute-done.49 = f32[44,512]{1,0:T(8,128)S(1)} collective-permute-done((f32[44,512]{1,0:T(8,128)S(1)}, f32[44,512]{1,0:T(8,128)S(1)}, u32[]{:S(2)}, u32[]{:S(2)}) %collective-permute-start.49) | collective-permute-done | bytes 90144 | tf_op jit(solution)/shard_map/ppermute | solution.py:42
  527.5 6.6 %collective-permute-done.52 = f32[176,512]{1,0:T(8,128)S(1)} collective-permute-done((f32[176,512]{1,0:T(8,128)S(1)}, f32[176,512]{1,0:T(8,128)S(1)}, u32[]{:S(2)}, u32[]{:S(2)}) %collective-permute-start.52) | collective-permute-done | bytes 360480 | tf_op jit(solution)/shard_map/ppermute | solution.py:42
  536.6 8.7 %collective-permute-done.17 = f32[64,2048]{1,0:T(8,128)S(1)} collective-permute-done((f32[64,2048]{1,0:T(8,128)S(1)}, f32[64,2048]{1,0:T(8,128)S(1)}, u32[]{:S(2)}, u32[]{:S(2)}) %collective-permute-start.17) | collective-permute-done | bytes 524320 | tf_op jit(solution)/shard_map/ppermute | solution.py:42
  547.7 5.8 collective-permute-done.18
  555.7 5.0 collective-permute-done.28
  560.9 3.0 collective-permute-start.20
  563.9 3.3 collective-permute-done.29
  578.5 5.8 collective-permute-done.31
  589.2 18.3 %collective-permute-done.32 = f32[256,512]{1,0:T(8,128)S(1)} collective-permute-done((f32[256,512]{1,0:T(8,128)S(1)}, f32[256,512]{1,0:T(8,128)S(1)}, u32[]{:S(2)}, u32[]{:S(2)}) %collective-permute-start.32) | collective-permute-done | bytes 524320 | tf_op jit(solution)/shard_map/ppermute | solution.py:42
  610.4 12.1 %collective-permute-done.33 = f32[512,512]{1,0:T(8,128)S(1)} collective-permute-done((f32[512,512]{1,0:T(8,128)S(1)}, f32[512,512]{1,0:T(8,128)S(1)}, u32[]{:S(2)}, u32[]{:S(2)}) %collective-permute-start.33) | collective-permute-done | bytes 1048608 | tf_op jit(solution)/shard_map/ppermute | solution.py:42
  633.6 4.8 copy.177
  (732 shorter events, 254.5 us)
Async XLA Ops:
  7.2 626.4 %all-reduce.26.cloned.1.call-start = ((), (), s32[]{:S(2)}) async-start(), calls=%async_computation | async-start | bytes 16777216 | tf_op jit(solution)/shard_map/psum | solution.py:486
  96.5 4.5 collective-permute-start.1
  101.1 3.7 collective-permute-start.2
  104.9 3.8 collective-permute-start.3
  108.7 5.8 collective-permute-start.4
  158.4 3.7 collective-permute-start.6
  162.2 8.8 %collective-permute-start.7 = (f32[2,512]{1,0:T(2,128)S(1)}, f32[2,512]{1,0:T(2,128)S(1)}, u32[]{:S(2)}, u32[]{:S(2)}) collective-permute-start(f32[2,512]{1,0:T(2,128)S(1)} %fusion.211), channel_id=1, source_target_pairs={{0,16},{4,20},{8,24},{12,28},{16,0},{20,4},{24,8},{28,12},{1,17},{... | collective-permute-start | bytes 12296 | tf_op jit(solution)/shard_map/ppermute | solution.py:42
  171.0 6.1 collective-permute-start.8
  177.1 9.5 %collective-permute-start.9 = (f32[2,512]{1,0:T(2,128)S(1)}, f32[2,512]{1,0:T(2,128)S(1)}, u32[]{:S(2)}, u32[]{:S(2)}) collective-permute-start(f32[2,512]{1,0:T(2,128)S(1)} %add.696), channel_id=1, source_target_pairs={{0,2},{1,3},{2,0},{3,1},{4,6},{5,7},{6,4},{7,5},{8,10},{9,11},{10,... | collective-permute-start | bytes 12296 | tf_op jit(solution)/shard_map/ppermute | solution.py:42
  365.5 16.6 %collective-permute-start.35 = (f32[448,512]{1,0:T(8,128)}, f32[448,512]{1,0:T(8,128)}, u32[]{:S(2)}, u32[]{:S(2)}) collective-permute-start(f32[448,512]{1,0:T(8,128)} %constant_dynamic-slice_fusion.14), channel_id=1, source_target_pairs={{0,4},{4,0},{8,12},{12,8},{16,20},{20,16},{24,28},{28,24},{1,5},{5... | collective-permute-start | bytes 2752520 | tf_op jit(solution)/shard_map/ppermute | solution.py:42
  371.5 6.7 %collective-permute-start.10 = (f32[7,512]{1,0:T(8,128)S(1)}, f32[7,512]{1,0:T(8,128)S(1)}, u32[]{:S(2)}, u32[]{:S(2)}) collective-permute-start(f32[7,512]{1,0:T(8,128)S(1)} %pad_maximum_fusion.33), channel_id=1, source_target_pairs={{0,4},{4,0},{8,12},{12,8},{16,20},{20,16},{24,28},{28,24},{1,5},{5... | collective-permute-start | bytes 43016 | tf_op jit(solution)/shard_map/ppermute | solution.py:42
  377.8 38.9 %collective-permute-start.45 = (f32[704,512]{1,0:T(8,128)}, f32[704,512]{1,0:T(8,128)}, u32[]{:S(2)}, u32[]{:S(2)}) collective-permute-start(f32[704,512]{1,0:T(8,128)} %constant_dynamic-slice_fusion.9), channel_id=1, source_target_pairs={{0,4},{4,0},{8,12},{12,8},{16,20},{20,16},{24,28},{28,24},{1,5},{5... | collective-permute-start | bytes 4325384 | tf_op jit(solution)/shard_map/ppermute | solution.py:42
  378.3 49.1 %collective-permute-start.55 = (f32[704,512]{1,0:T(8,128)}, f32[704,512]{1,0:T(8,128)}, u32[]{:S(2)}, u32[]{:S(2)}) collective-permute-start(f32[704,512]{1,0:T(8,128)} %constant_dynamic-slice_fusion.4), channel_id=1, source_target_pairs={{0,4},{4,0},{8,12},{12,8},{16,20},{20,16},{24,28},{28,24},{1,5},{5... | collective-permute-start | bytes 4325384 | tf_op jit(solution)/shard_map/ppermute | solution.py:42
  378.3 3.8 collective-permute-start.11
  382.1 3.7 collective-permute-start.12
  383.6 16.9 %collective-permute-start.36 = (f32[224,512]{1,0:T(8,128)S(1)}, f32[224,512]{1,0:T(8,128)}, u32[]{:S(2)}, u32[]{:S(2)}) collective-permute-start(f32[224,512]{1,0:T(8,128)S(1)} %constant_dynamic-slice_fusion.13), channel_id=1, source_target_pairs={{0,1},{1,0},{2,3},{3,2},{4,5},{5,4},{6,7},{7,6},{8,9},{9,8},{10,11... | collective-permute-start | bytes 1376264 | tf_op jit(solution)/shard_map/ppermute | solution.py:42
  385.9 9.9 %collective-permute-start.13 = (f32[7,512]{1,0:T(8,128)S(1)}, f32[7,512]{1,0:T(8,128)S(1)}, u32[]{:S(2)}, u32[]{:S(2)}) collective-permute-start(f32[7,512]{1,0:T(8,128)S(1)} %add.710), channel_id=1, source_target_pairs={{0,1},{1,0},{2,3},{3,2},{4,5},{5,4},{6,7},{7,6},{8,9},{9,8},{10,11... | collective-permute-start | bytes 43016 | tf_op jit(solution)/shard_map/ppermute | solution.py:42
  389.8 58.0 %collective-permute-start.15 = (f32[256,2048]{1,0:T(8,128)}, f32[256,2048]{1,0:T(8,128)S(1)}, u32[]{:S(2)}, u32[]{:S(2)}) collective-permute-start(f32[256,2048]{1,0:T(8,128)} %constant_dynamic-slice_fusion.24), channel_id=1, source_target_pairs={{0,4},{4,0},{8,12},{12,8},{16,20},{20,16},{24,28},{28,24},{1,5},{5... | collective-permute-start | bytes 6291464 | tf_op jit(solution)/shard_map/ppermute | solution.py:42
  395.8 4.6 collective-permute-start.14
  400.4 48.7 %collective-permute-start.25 = (f32[1024,512]{1,0:T(8,128)S(1)}, f32[1024,512]{1,0:T(8,128)S(1)}, u32[]{:S(2)}, u32[]{:S(2)}) collective-permute-start(f32[1024,512]{1,0:T(8,128)S(1)} %constant_dynamic-slice_fusion.19), channel_id=1, source_target_pairs={{0,4},{4,0},{8,12},{12,8},{16,20},{20,16},{24,28},{28,24},{1,5},{5... | collective-permute-start | bytes 6291464 | tf_op jit(solution)/shard_map/ppermute | solution.py:42
  401.6 13.7 %collective-permute-start.37 = (f32[112,512]{1,0:T(8,128)S(1)}, f32[112,512]{1,0:T(8,128)S(1)}, u32[]{:S(2)}, u32[]{:S(2)}) collective-permute-start(f32[112,512]{1,0:T(8,128)S(1)} %constant_dynamic-slice_fusion.12), channel_id=1, source_target_pairs={{0,2},{1,3},{2,0},{3,1},{4,6},{5,7},{6,4},{7,5},{8,10},{9,11},{10,... | collective-permute-start | bytes 688136 | tf_op jit(solution)/shard_map/ppermute | solution.py:42
  415.3 5.2 collective-permute-start.38
  420.5 5.0 collective-permute-start.39
  422.3 29.0 %collective-permute-start.46 = (f32[352,512]{1,0:T(8,128)S(1)}, f32[352,512]{1,0:T(8,128)S(1)}, u32[]{:S(2)}, u32[]{:S(2)}) collective-permute-start(f32[352,512]{1,0:T(8,128)S(1)} %constant_dynamic-slice_fusion.8), channel_id=1, source_target_pairs={{0,16},{4,20},{8,24},{12,28},{16,0},{20,4},{24,8},{28,12},{1,17},{... | collective-permute-start | bytes 2162696 | tf_op jit(solution)/shard_map/ppermute | solution.py:42
  425.6 15.9 %collective-permute-start.40 = (f32[28,512]{1,0:T(8,128)S(1)}, f32[28,512]{1,0:T(8,128)S(1)}, u32[]{:S(2)}, u32[]{:S(2)}) collective-permute-start(f32[28,512]{1,0:T(8,128)S(1)} %dynamic-slice_add_fusion.24), channel_id=1, source_target_pairs={{0,16},{4,20},{8,24},{12,28},{16,0},{20,4},{24,8},{28,12},{1,17},{... | collective-permute-start | bytes 172040 | tf_op jit(solution)/shard_map/ppermute | solution.py:42
  441.5 6.1 collective-permute-start.41
  442.3 20.8 %collective-permute-start.56 = (f32[352,512]{1,0:T(8,128)S(1)}, f32[352,512]{1,0:T(8,128)S(1)}, u32[]{:S(2)}, u32[]{:S(2)}) collective-permute-start(f32[352,512]{1,0:T(8,128)S(1)} %constant_dynamic-slice_fusion.3), channel_id=1, source_target_pairs={{0,8},{4,12},{8,0},{12,4},{16,24},{20,28},{24,16},{28,20},{1,9},{5... | collective-permute-start | bytes 2162696 | tf_op jit(solution)/shard_map/ppermute | solution.py:42
  447.7 16.5 %collective-permute-start.42 = (f32[112,512]{1,0:T(8,128)S(1)}, f32[112,512]{1,0:T(8,128)S(1)}, u32[]{:S(2)}, u32[]{:S(2)}) collective-permute-start(f32[112,512]{1,0:T(8,128)S(1)} %pad_maximum_fusion.29), channel_id=1, source_target_pairs={{0,2},{1,3},{2,0},{3,1},{4,6},{5,7},{6,4},{7,5},{8,10},{9,11},{10,... | collective-permute-start | bytes 688136 | tf_op jit(solution)/shard_map/ppermute | solution.py:42
  448.2 76.0 %collective-permute-start.16 = (f32[128,2048]{1,0:T(8,128)S(1)}, f32[128,2048]{1,0:T(8,128)S(1)}, u32[]{:S(2)}, u32[]{:S(2)}) collective-permute-start(f32[128,2048]{1,0:T(8,128)S(1)} %constant_dynamic-slice_fusion.23), channel_id=1, source_target_pairs={{0,16},{4,20},{8,24},{12,28},{16,0},{20,4},{24,8},{28,12},{1,17},{... | collective-permute-start | bytes 3145736 | tf_op jit(solution)/shard_map/ppermute | solution.py:42
  450.6 74.6 %collective-permute-start.26 = (f32[512,512]{1,0:T(8,128)S(1)}, f32[512,512]{1,0:T(8,128)S(1)}, u32[]{:S(2)}, u32[]{:S(2)}) collective-permute-start(f32[512,512]{1,0:T(8,128)S(1)} %constant_dynamic-slice_fusion.18), channel_id=1, source_target_pairs={{0,8},{4,12},{8,0},{12,4},{16,24},{20,28},{24,16},{28,20},{1,9},{5... | collective-permute-start | bytes 3145736 | tf_op jit(solution)/shard_map/ppermute | solution.py:42
  451.5 39.5 %collective-permute-start.47 = (f32[176,512]{1,0:T(8,128)S(1)}, f32[176,512]{1,0:T(8,128)S(1)}, u32[]{:S(2)}, u32[]{:S(2)}) collective-permute-start(f32[176,512]{1,0:T(8,128)S(1)} %constant_dynamic-slice_fusion.7), channel_id=1, source_target_pairs={{0,8},{4,12},{8,0},{12,4},{16,24},{20,28},{24,16},{28,20},{1,9},{5... | collective-permute-start | bytes 1081352 | tf_op jit(solution)/shard_map/ppermute | solution.py:42
  463.3 27.9 %collective-permute-start.57 = (f32[176,512]{1,0:T(8,128)S(1)}, f32[176,512]{1,0:T(8,128)S(1)}, u32[]{:S(2)}, u32[]{:S(2)}) collective-permute-start(f32[176,512]{1,0:T(8,128)S(1)} %constant_dynamic-slice_fusion.2), channel_id=1, source_target_pairs={{0,16},{4,20},{8,24},{12,28},{16,0},{20,4},{24,8},{28,12},{1,17},{... | collective-permute-start | bytes 1081352 | tf_op jit(solution)/shard_map/ppermute | solution.py:42
  464.3 52.8 %collective-permute-start.43 = (f32[224,512]{1,0:T(8,128)S(1)}, f32[224,512]{1,0:T(8,128)S(1)}, u32[]{:S(2)}, u32[]{:S(2)}) collective-permute-start(f32[224,512]{1,0:T(8,128)S(1)} %pad_maximum_fusion.24), channel_id=1, source_target_pairs={{0,1},{1,0},{2,3},{3,2},{4,5},{5,4},{6,7},{7,6},{8,9},{9,8},{10,11... | collective-permute-start | bytes 1376264 | tf_op jit(solution)/shard_map/ppermute | solution.py:42
  491.1 6.7 %collective-permute-start.48 = (f32[88,512]{1,0:T(8,128)S(1)}, f32[88,512]{1,0:T(8,128)S(1)}, u32[]{:S(2)}, u32[]{:S(2)}) collective-permute-start(f32[88,512]{1,0:T(8,128)S(1)} %constant_dynamic-slice_fusion.6), channel_id=1, source_target_pairs={{0,1},{1,0},{2,3},{3,2},{4,5},{5,4},{6,7},{7,6},{8,9},{9,8},{10,11... | collective-permute-start | bytes 540680 | tf_op jit(solution)/shard_map/ppermute | solution.py:42
  491.3 9.2 %collective-permute-start.58 = (f32[88,512]{1,0:T(8,128)S(1)}, f32[88,512]{1,0:T(8,128)S(1)}, u32[]{:S(2)}, u32[]{:S(2)}) collective-permute-start(f32[88,512]{1,0:T(8,128)S(1)} %constant_dynamic-slice_fusion.1), channel_id=1, source_target_pairs={{0,1},{1,0},{2,3},{3,2},{4,5},{5,4},{6,7},{7,6},{8,9},{9,8},{10,11... | collective-permute-start | bytes 540680 | tf_op jit(solution)/shard_map/ppermute | solution.py:42
  497.8 10.7 %collective-permute-start.49 = (f32[44,512]{1,0:T(8,128)S(1)}, f32[44,512]{1,0:T(8,128)S(1)}, u32[]{:S(2)}, u32[]{:S(2)}) collective-permute-start(f32[44,512]{1,0:T(8,128)S(1)} %constant_dynamic-slice_fusion.5), channel_id=1, source_target_pairs={{0,2},{1,3},{2,0},{3,1},{4,6},{5,7},{6,4},{7,5},{8,10},{9,11},{10,... | collective-permute-start | bytes 270344 | tf_op jit(solution)/shard_map/ppermute | solution.py:42
  500.5 10.1 %collective-permute-start.59 = (f32[44,512]{1,0:T(8,128)S(1)}, f32[44,512]{1,0:T(8,128)S(1)}, u32[]{:S(2)}, u32[]{:S(2)}) collective-permute-start(f32[44,512]{1,0:T(8,128)S(1)} %constant_dynamic-slice_fusion), channel_id=1, source_target_pairs={{0,2},{1,3},{2,0},{3,1},{4,6},{5,7},{6,4},{7,5},{8,10},{9,11},{10,... | collective-permute-start | bytes 270344 | tf_op jit(solution)/shard_map/ppermute | solution.py:42
  508.6 5.7 collective-permute-start.50
  510.7 6.2 collective-permute-start.60
  514.4 5.6 collective-permute-start.51
  517.0 5.6 collective-permute-start.61
  517.2 19.2 %collective-permute-start.44 = (f32[448,512]{1,0:T(8,128)S(1)}, f32[448,512]{1,0:T(8,128)S(1)}, u32[]{:S(2)}, u32[]{:S(2)}) collective-permute-start(f32[448,512]{1,0:T(8,128)S(1)} %pad_maximum_fusion.19), channel_id=1, source_target_pairs={{0,4},{4,0},{8,12},{12,8},{16,20},{20,16},{24,28},{28,24},{1,5},{5... | collective-permute-start | bytes 2752520 | tf_op jit(solution)/shard_map/ppermute | solution.py:42
  522.6 11.4 %collective-permute-start.52 = (f32[176,512]{1,0:T(8,128)S(1)}, f32[176,512]{1,0:T(8,128)S(1)}, u32[]{:S(2)}, u32[]{:S(2)}) collective-permute-start(f32[176,512]{1,0:T(8,128)S(1)} %pad_maximum_fusion.25), channel_id=1, source_target_pairs={{0,8},{4,12},{8,0},{12,4},{16,24},{20,28},{24,16},{28,20},{1,9},{5... | collective-permute-start | bytes 1081352 | tf_op jit(solution)/shard_map/ppermute | solution.py:42
  523.5 11.4 %collective-permute-start.62 = (f32[176,512]{1,0:T(8,128)S(1)}, f32[176,512]{1,0:T(8,128)S(1)}, u32[]{:S(2)}, u32[]{:S(2)}) collective-permute-start(f32[176,512]{1,0:T(8,128)S(1)} %pad_maximum_fusion.26), channel_id=1, source_target_pairs={{0,16},{4,20},{8,24},{12,28},{16,0},{20,4},{24,8},{28,12},{1,17},{... | collective-permute-start | bytes 1081352 | tf_op jit(solution)/shard_map/ppermute | solution.py:42
  524.3 20.9 %collective-permute-start.17 = (f32[64,2048]{1,0:T(8,128)S(1)}, f32[64,2048]{1,0:T(8,128)S(1)}, u32[]{:S(2)}, u32[]{:S(2)}) collective-permute-start(f32[64,2048]{1,0:T(8,128)S(1)} %constant_dynamic-slice_fusion.22), channel_id=1, source_target_pairs={{0,8},{4,12},{8,0},{12,4},{16,24},{20,28},{24,16},{28,20},{1,9},{5... | collective-permute-start | bytes 1572872 | tf_op jit(solution)/shard_map/ppermute | solution.py:42
  525.4 20.7 %collective-permute-start.27 = (f32[256,512]{1,0:T(8,128)S(1)}, f32[256,512]{1,0:T(8,128)S(1)}, u32[]{:S(2)}, u32[]{:S(2)}) collective-permute-start(f32[256,512]{1,0:T(8,128)S(1)} %constant_dynamic-slice_fusion.17), channel_id=1, source_target_pairs={{0,16},{4,20},{8,24},{12,28},{16,0},{20,4},{24,8},{28,12},{1,17},{... | collective-permute-start | bytes 1572872 | tf_op jit(solution)/shard_map/ppermute | solution.py:42
  534.2 44.1 %collective-permute-start.53 = (f32[352,512]{1,0:T(8,128)S(1)}, f32[352,512]{1,0:T(8,128)S(1)}, u32[]{:S(2)}, u32[]{:S(2)}) collective-permute-start(f32[352,512]{1,0:T(8,128)S(1)} %pad_maximum_fusion.20), channel_id=1, source_target_pairs={{0,16},{4,20},{8,24},{12,28},{16,0},{20,4},{24,8},{28,12},{1,17},{... | collective-permute-start | bytes 2162696 | tf_op jit(solution)/shard_map/ppermute | solution.py:42
  535.0 53.3 %collective-permute-start.63 = (f32[352,512]{1,0:T(8,128)S(1)}, f32[352,512]{1,0:T(8,128)S(1)}, u32[]{:S(2)}, u32[]{:S(2)}) collective-permute-start(f32[352,512]{1,0:T(8,128)S(1)} %pad_maximum_fusion.21), channel_id=1, source_target_pairs={{0,8},{4,12},{8,0},{12,4},{16,24},{20,28},{24,16},{28,20},{1,9},{5... | collective-permute-start | bytes 2162696 | tf_op jit(solution)/shard_map/ppermute | solution.py:42
  545.4 8.1 %collective-permute-start.18 = (f32[32,2048]{1,0:T(8,128)S(1)}, f32[32,2048]{1,0:T(8,128)S(1)}, u32[]{:S(2)}, u32[]{:S(2)}) collective-permute-start(f32[32,2048]{1,0:T(8,128)S(1)} %constant_dynamic-slice_fusion.21), channel_id=1, source_target_pairs={{0,1},{1,0},{2,3},{3,2},{4,5},{5,4},{6,7},{7,6},{8,9},{9,8},{10,11... | collective-permute-start | bytes 786440 | tf_op jit(solution)/shard_map/ppermute | solution.py:42
  546.3 14.5 %collective-permute-start.28 = (f32[128,512]{1,0:T(8,128)S(1)}, f32[128,512]{1,0:T(8,128)S(1)}, u32[]{:S(2)}, u32[]{:S(2)}) collective-permute-start(f32[128,512]{1,0:T(8,128)S(1)} %constant_dynamic-slice_fusion.16), channel_id=1, source_target_pairs={{0,1},{1,0},{2,3},{3,2},{4,5},{5,4},{6,7},{7,6},{8,9},{9,8},{10,11... | collective-permute-start | bytes 786440 | tf_op jit(solution)/shard_map/ppermute | solution.py:42
  553.6 7.3 %collective-permute-start.19 = (f32[16,2048]{1,0:T(8,128)S(1)}, f32[16,2048]{1,0:T(8,128)S(1)}, u32[]{:S(2)}, u32[]{:S(2)}) collective-permute-start(f32[16,2048]{1,0:T(8,128)S(1)} %constant_dynamic-slice_fusion.20), channel_id=1, source_target_pairs={{0,2},{1,3},{2,0},{3,1},{4,6},{5,7},{6,4},{7,5},{8,10},{9,11},{10,... | collective-permute-start | bytes 393224 | tf_op jit(solution)/shard_map/ppermute | solution.py:42
  560.8 6.4 collective-permute-start.29
  560.9 8.7 %collective-permute-start.20 = (f32[16,2048]{1,0:T(8,128)S(1)}, f32[16,2048]{1,0:T(8,128)S(1)}, u32[]{:S(2)}, u32[]{:S(2)}) collective-permute-start(f32[16,2048]{1,0:T(8,128)S(1)} %dynamic-slice_add_fusion.20), channel_id=1, source_target_pairs={{0,2},{1,3},{2,0},{3,1},{4,6},{5,7},{6,4},{7,5},{8,10},{9,11},{10,... | collective-permute-start | bytes 393224 | tf_op jit(solution)/shard_map/ppermute | solution.py:42
  567.2 6.4 collective-permute-start.30
  569.7 6.7 %collective-permute-start.21 = (f32[32,2048]{1,0:T(8,128)S(1)}, f32[32,2048]{1,0:T(8,128)S(1)}, u32[]{:S(2)}, u32[]{:S(2)}) collective-permute-start(f32[32,2048]{1,0:T(8,128)S(1)} %pad_maximum_fusion.27), channel_id=1, source_target_pairs={{0,1},{1,0},{2,3},{3,2},{4,5},{5,4},{6,7},{7,6},{8,9},{9,8},{10,11... | collective-permute-start | bytes 786440 | tf_op jit(solution)/shard_map/ppermute | solution.py:42
  576.5 9.2 %collective-permute-start.22 = (f32[64,2048]{1,0:T(8,128)S(1)}, f32[64,2048]{1,0:T(8,128)S(1)}, u32[]{:S(2)}, u32[]{:S(2)}) collective-permute-start(f32[64,2048]{1,0:T(8,128)S(1)} %pad_maximum_fusion.22), channel_id=1, source_target_pairs={{0,8},{4,12},{8,0},{12,4},{16,24},{20,28},{24,16},{28,20},{1,9},{5... | collective-permute-start | bytes 1572872 | tf_op jit(solution)/shard_map/ppermute | solution.py:42
  577.8 6.4 collective-permute-start.31
  585.9 22.8 %collective-permute-start.23 = (f32[128,2048]{1,0:T(8,128)S(1)}, f32[128,2048]{1,0:T(8,128)S(1)}, u32[]{:S(2)}, u32[]{:S(2)}) collective-permute-start(f32[128,2048]{1,0:T(8,128)S(1)} %pad_maximum_fusion.17), channel_id=1, source_target_pairs={{0,16},{4,20},{8,24},{12,28},{16,0},{20,4},{24,8},{28,12},{1,17},{... | collective-permute-start | bytes 3145736 | tf_op jit(solution)/shard_map/ppermute | solution.py:42
  586.5 20.9 %collective-permute-start.32 = (f32[256,512]{1,0:T(8,128)S(1)}, f32[256,512]{1,0:T(8,128)S(1)}, u32[]{:S(2)}, u32[]{:S(2)}) collective-permute-start(f32[256,512]{1,0:T(8,128)S(1)} %pad_maximum_fusion.23), channel_id=1, source_target_pairs={{0,16},{4,20},{8,24},{12,28},{16,0},{20,4},{24,8},{28,12},{1,17},{... | collective-permute-start | bytes 1572872 | tf_op jit(solution)/shard_map/ppermute | solution.py:42
  588.3 36.7 %collective-permute-start.54 = (f32[704,512]{1,0:T(8,128)S(1)}, f32[704,512]{1,0:T(8,128)S(1)}, u32[]{:S(2)}, u32[]{:S(2)}) collective-permute-start(f32[704,512]{1,0:T(8,128)S(1)} %pad_maximum_fusion.11), channel_id=1, source_target_pairs={{0,4},{4,0},{8,12},{12,8},{16,20},{20,16},{24,28},{28,24},{1,5},{5... | collective-permute-start | bytes 4325384 | tf_op jit(solution)/shard_map/ppermute | solution.py:42
  588.6 34.4 %collective-permute-start.64 = (f32[704,512]{1,0:T(8,128)S(1)}, f32[704,512]{1,0:T(8,128)S(1)}, u32[]{:S(2)}, u32[]{:S(2)}) collective-permute-start(f32[704,512]{1,0:T(8,128)S(1)} %pad_maximum_fusion.12), channel_id=1, source_target_pairs={{0,4},{4,0},{8,12},{12,8},{16,20},{20,16},{24,28},{28,24},{1,5},{5... | collective-permute-start | bytes 4325384 | tf_op jit(solution)/shard_map/ppermute | solution.py:42
  607.7 14.9 %collective-permute-start.33 = (f32[512,512]{1,0:T(8,128)S(1)}, f32[512,512]{1,0:T(8,128)S(1)}, u32[]{:S(2)}, u32[]{:S(2)}) collective-permute-start(f32[512,512]{1,0:T(8,128)S(1)} %pad_maximum_fusion.18), channel_id=1, source_target_pairs={{0,8},{4,12},{8,0},{12,4},{16,24},{20,28},{24,16},{28,20},{1,9},{5... | collective-permute-start | bytes 3145736 | tf_op jit(solution)/shard_map/ppermute | solution.py:42
  609.2 18.6 %collective-permute-start.24 = (f32[256,2048]{1,0:T(8,128)S(1)}, f32[256,2048]{1,0:T(8,128)S(1)}, u32[]{:S(2)}, u32[]{:S(2)}) collective-permute-start(f32[256,2048]{1,0:T(8,128)S(1)} %pad_maximum_fusion.8), channel_id=1, source_target_pairs={{0,4},{4,0},{8,12},{12,8},{16,20},{20,16},{24,28},{28,24},{1,5},{5... | collective-permute-start | bytes 6291464 | tf_op jit(solution)/shard_map/ppermute | solution.py:42
  622.9 7.7 %collective-permute-start.34 = (f32[1024,512]{1,0:T(8,128)S(1)}, f32[1024,512]{1,0:T(8,128)S(1)}, u32[]{:S(2)}, u32[]{:S(2)}) collective-permute-start(f32[1024,512]{1,0:T(8,128)S(1)} %pad_maximum_fusion.9), channel_id=1, source_target_pairs={{0,4},{4,0},{8,12},{12,8},{16,20},{20,16},{24,28},{28,24},{1,5},{5... | collective-permute-start | bytes 6291464 | tf_op jit(solution)/shard_map/ppermute | solution.py:42
  (175 other events, 1065.7 us)
Sparse Core Ops, SparseCore 0:
  186.8 177.1 all-reduce.25

commit v2 on v0

v2 whole, which is shorter than its diff:
```python
import jax
import jax.numpy as jnp
from jax import lax
from jax.experimental import pallas as pl
from jax.experimental.pallas import tpu as pltpu
from jax.sharding import PartitionSpec as P

HEADS = 8
HEAD = 64
LANES = 128
TILE = 256
EPSILON = 1e-05
AXES = ("dp", "stream")
F32 = jnp.float32
LOW = jnp.bfloat16

(
    GAIN_ONE,
    SHIFT_ONE,
    OFFSET_ONE,
    ATTEND_GAIN,
    ATTEND_SHIFT,
    QUERY_BIAS,
    VALUE_BIAS,
    OUTPUT_BIAS,
    MIXING_GAIN,
    MIXING_SHIFT,
    BATCH_GAIN,
    BATCH_SHIFT,
    SECOND_BIAS,
    GAIN_TWO,
    SHIFT_TWO,
    OFFSET_TWO,
    FINAL_GAIN,
    FINAL_SHIFT,
    FIRST_BIAS,
) = range(19)
TAPS = 20


def nn(a, b):
    return lax.dot_general(a, b, (((1,), (0,)), ((), ())), preferred_element_type=F32)


def nt(a, b):
    return lax.dot_general(a, b, (((1,), (1,)), ((), ())), preferred_element_type=F32)


def tn(a, b):
    return lax.dot_general(a, b, (((0,), (0,)), ((), ())), preferred_element_type=F32)


def column_sum(values):
    return jnp.sum(values, axis=0, keepdims=True)


def sigmoid(values):
    return 0.5 * jnp.tanh(0.5 * values) + 0.5


def normalize(values):
    centred = values - jnp.mean(values, axis=-1, keepdims=True)
    spread = jnp.mean(centred * centred, axis=-1, keepdims=True)
    scale = lax.rsqrt(spread + EPSILON)
    return centred * scale, scale


def norm_backward(grad, gain, unit, scale):
    inner = grad * gain
    middle = jnp.mean(inner, axis=-1, keepdims=True)
    tilt = jnp.mean(inner * unit, axis=-1, keepdims=True)
    return scale * (inner - middle - unit * tilt)


def row_of(table, at, count=1):
    return table[at : at + count, :]


def valid_rows(lengths_ref, step, rows):
    at = lax.broadcasted_iota(jnp.int32, (rows, 1), 0) + step * rows
    return (at < lengths_ref[0]).astype(F32)


def split_three(values):
    high = values.astype(LOW).astype(F32)
    rest = values - high
    middle = rest.astype(LOW).astype(F32)
    return high, middle, rest - middle


def gather_rows(ref, at, rows):
    for offset, row in enumerate(rows):
        ref[at + offset : at + offset + 1, :] += row


def lane_index(rows):
    return lax.broadcasted_iota(jnp.int32, (rows, LANES), 1)


def head_lanes(values, head):
    pair = values[:, (head // 2) * LANES : (head // 2 + 1) * LANES]
    if head % 2 == 1:
        pair = pltpu.roll(pair, HEAD, 1)
    return pair


def join_pair(even, odd):
    lanes = lane_index(even.shape[0])
    return jnp.where(lanes < HEAD, even, pltpu.roll(odd, HEAD, 1))


def front_kernel(
    lengths, x, table, lift, expand, reducer, query, key, value,
    normed_a, acted, slope, x1, normed_b, queries, keys, values, sums,
):
    step = pl.program_id(0)

    @pl.when(step == 0)
    def _():
        sums[...] = jnp.zeros_like(sums)

    rows = x.shape[0]
    valid = valid_rows(lengths, step, rows)
    x0 = x[...].astype(F32)
    unit, scale = normalize(x0)
    low = (unit * row_of(table, GAIN_ONE) + row_of(table, SHIFT_ONE)).astype(LOW)
    normed_a[...] = low
    width = 512
    branch = jnp.zeros((rows, x.shape[1]), F32)
    for part in range(expand.shape[1] // width):
        cut = slice(part * width, (part + 1) * width)
        inner = nn(low, expand[:, cut]) + lift[:, cut]
        gate = sigmoid(inner)
        silu = inner * gate
        active = silu.astype(LOW)
        acted[:, cut] = active
        slope[:, cut] = (gate + silu * (1.0 - gate)).astype(LOW)
        branch = branch + nn(active, reducer[cut, :])
    branch = 0.5 * (branch + row_of(table, OFFSET_ONE))
    after = x0 + branch
    x1[...] = after
    gather_rows(sums, 0, [column_sum(valid * after * after), column_sum(valid * branch * branch)])
    unit, scale = normalize(after)
    low = (unit * row_of(table, ATTEND_GAIN) + row_of(table, ATTEND_SHIFT)).astype(LOW)
    normed_b[...] = low
    lanes = lane_index(rows)
    q_all = (nn(low, query[...]) + row_of(table, QUERY_BIAS)).astype(LOW).astype(F32) * HEAD ** (-0.5)
    k_all = nn(low, key[...])
    v_all = nn(low, value[...]) + row_of(table, VALUE_BIAS)
    ones = jnp.where((lanes >= HEAD) & (lanes < HEAD + 4), 1.0, 0.0)
    first = jnp.where(lanes == HEAD, 1.0, 0.0)
    shade = jnp.where(lanes == HEAD, (valid - 1.0) * 1e30, ones)
    for head in range(HEADS):
        queries[head, :, :] = jnp.where(lanes < HEAD, head_lanes(q_all, head), first).astype(LOW)
        keys[head, :, :] = jnp.where(lanes < HEAD, head_lanes(k_all, head), shade).astype(LOW)
        values[head, :, :] = jnp.where(lanes < HEAD, head_lanes(v_all, head), ones).astype(LOW)


def attend_kernel(
    lengths, queries, keys, values, x1, table, output, point,
    again, mixed_wide, mixed, x2, normed_c, gated, gate_out, convolved, moments, sums,
    padded,
):
    step = pl.program_id(0)
    steps = pl.num_programs(0)
    rows = x1.shape[0]
    width = x1.shape[1]

    @pl.when(step == 0)
    def _():
        sums[...] = jnp.zeros_like(sums)
        padded[0:8, :] = jnp.zeros((8, width), F32)
        padded[padded.shape[0] - 8 :, :] = jnp.zeros((8, width), F32)

    valid = valid_rows(lengths, step, rows)
    lanes = lane_index(rows)
    found = []
    for head in range(HEADS):
        query = queries[head, :, :]
        scores = nt(query, keys[head, :, :])
        top = jnp.max(scores, axis=-1, keepdims=True)
        raised = jnp.exp(scores - top).astype(LOW)
        blend = nn(raised, values[head, :, :])
        total = blend[:, HEAD : HEAD + 1]
        found.append(blend * (1.0 / total))
        high, middle, rest = split_three(-(top + jnp.log(total)))
        marked = jnp.where(lanes == HEAD + 1, high, query.astype(F32))
        marked = jnp.where(lanes == HEAD + 2, middle, marked)
        again[head, :, :] = jnp.where(lanes == HEAD + 3, rest, marked).astype(LOW)
    wide = jnp.concatenate(
        [join_pair(found[2 * pair], found[2 * pair + 1]) for pair in range(HEADS // 2)], axis=1
    )
    mixed_wide[...] = wide
    low = wide.astype(LOW)
    mixed[...] = low
    branch = nn(low, output[...]) + row_of(table, OUTPUT_BIAS)
    after = x1[...] + branch
    x2[...] = after
    gather_rows(sums, 0, [column_sum(valid * after * after), column_sum(valid * branch * branch)])
    unit, scale = normalize(after)
    low = (unit * row_of(table, MIXING_GAIN) + row_of(table, MIXING_SHIFT)).astype(LOW)
    normed_c[...] = low
    doubled = nn(low, point[...])
    gate = sigmoid(doubled[:, width:] + row_of(table, FIRST_BIAS + 1))
    passed = (doubled[:, :width] + row_of(table, FIRST_BIAS)) * gate * valid
    gated[...] = passed
    gate_out[...] = gate
    padded[pl.ds(pl.multiple_of(8 + step * rows, 8), rows), :] = passed

    @pl.when(step == steps - 1)
    def _():
        frames = convolved.shape[0]
        chunk = 128
        count = lengths[0].astype(F32)
        summed = jnp.zeros((1, width), F32)
        for part in range(frames // chunk):
            total = jnp.zeros((chunk, width), F32)
            for tap in range(9):
                start = part * chunk + 4 + tap
                total = total + padded[start : start + chunk, :] * row_of(table, TAPS + tap)
            convolved[part * chunk : (part + 1) * chunk, :] = total
            here = lax.broadcasted_iota(jnp.int32, (chunk, 1), 0) + part * chunk < lengths[0]
            summed = summed + column_sum(jnp.where(here, total, 0.0))
        mean = summed / count
        spread = jnp.zeros((1, width), F32)
        for part in range(frames // chunk):
            here = lax.broadcasted_iota(jnp.int32, (chunk, 1), 0) + part * chunk < lengths[0]
            apart = jnp.where(here, convolved[part * chunk : (part + 1) * chunk, :] - mean, 0.0)
            spread = spread + column_sum(apart * apart)
        moments[...] = jnp.zeros_like(moments)
        moments[0:1, :] = jnp.full((1, width), count, F32)
        moments[1:2, :] = summed
        moments[2:3, :] = spread


def rear_kernel(
    lengths, convolved, x2, cotangent, moments, table, lift, second, expand, reducer,
    block_output, acted_c, low_c, acted, half_low, normed_d, inner_low, stream, direct, sums, wide_sums,
):
    step = pl.program_id(0)

    @pl.when(step == 0)
    def _():
        sums[...] = jnp.zeros_like(sums)
        wide_sums[...] = jnp.zeros_like(wide_sums)

    rows = x2.shape[0]
    valid = valid_rows(lengths, step, rows)
    mean = moments[1:2, :] / moments[0:1, :]
    inverse = lax.rsqrt(moments[2:3, :] / moments[0:1, :] + EPSILON)
    unit_c = (convolved[...] - mean) * inverse
    normal = unit_c * row_of(table, BATCH_GAIN) + row_of(table, BATCH_SHIFT)
    gate = sigmoid(normal)
    silu = normal * gate
    slope_c = gate + silu * (1.0 - gate)
    active_c = silu.astype(LOW)
    acted_c[...] = active_c
    branch = nn(active_c, second[...]) + row_of(table, SECOND_BIAS)
    x3 = x2[...] + branch
    squares = [column_sum(valid * x3 * x3), column_sum(valid * branch * branch)]
    unit_d, scale_d = normalize(x3)
    low_d = (unit_d * row_of(table, GAIN_TWO) + row_of(table, SHIFT_TWO)).astype(LOW)
    normed_d[...] = low_d
    width = 512
    parts = expand.shape[1] // width
    branch = jnp.zeros_like(x3)
    slopes = []
    for part in range(parts):
        cut = slice(part * width, (part + 1) * width)
        inner = nn(low_d, expand[:, cut]) + lift[:, cut]
        gate = sigmoid(inner)
        silu = inner * gate
        active = silu.astype(LOW)
        acted[:, cut] = active
        slopes.append((gate + silu * (1.0 - gate)).astype(LOW))
        branch = branch + nn(active, reducer[cut, :])
    branch = 0.5 * (branch + row_of(table, OFFSET_TWO))
    x4 = x3 + branch
    squares += [column_sum(valid * x4 * x4), column_sum(valid * branch * branch)]
    unit, scale = normalize(x4)
    gain = row_of(table, FINAL_GAIN)
    block_output[...] = (valid * (unit * gain + row_of(table, FINAL_SHIFT))).astype(LOW)
    grad = cotangent[...].astype(F32) * valid
    closing = [column_sum(grad * unit), column_sum(grad)]
    g4 = norm_backward(grad, gain, unit, scale)
    low = (0.5 * g4).astype(LOW)
    half_low[...] = low
    back = jnp.zeros_like(x3)
    for part in range(parts):
        cut = slice(part * width, (part + 1) * width)
        inner = (nt(low, reducer[cut, :]) * slopes[part].astype(F32)).astype(LOW)
        inner_low[:, cut] = inner
        wide_sums[part : part + 1, :] += column_sum(inner.astype(F32))
        back = back + nt(inner, expand[:, cut])
    second_sums = [column_sum(back * unit_d), column_sum(back), column_sum(low.astype(F32))]
    g3 = g4 + norm_backward(back, row_of(table, GAIN_TWO), unit_d, scale_d)
    stream[...] = g3
    low = g3.astype(LOW)
    low_c[...] = low
    grad = nt(low, second[...]) * slope_c
    direct[...] = grad * (row_of(table, BATCH_GAIN) * inverse)
    gather_rows(
        sums,
        0,
        [column_sum(grad), column_sum(grad * unit_c), column_sum(low.astype(F32))]
        + second_sums
        + closing
        + squares,
    )


def weight_kernel(pairs):
    def kernel(*refs):
        for at in range(pairs):
            refs[2 * pairs + at][...] = tn(refs[2 * at][...], refs[2 * at + 1][...])

    return kernel


def mixing_kernel(
    lengths, moments, batch_sums, direct, convolved, gated, gate, x2, stream, mixed_wide, table, point, output,
    doubled_low, stream_out, out_low, grads, sums,
    padded,
):
    step = pl.program_id(0)
    rows = x2.shape[0]
    width = x2.shape[1]
    frames = direct.shape[0]

    @pl.when(step == 0)
    def _():
        sums[...] = jnp.zeros_like(sums)
        count = moments[0:1, :]
        mean = moments[1:2, :] / count
        inverse = lax.rsqrt(moments[2:3, :] / count + EPSILON)
        weight = row_of(table, BATCH_GAIN) * inverse
        mean_grad = -weight * batch_sums[0:1, :] / count
        var_grad = -(inverse * weight) * batch_sums[1:2, :] / count
        padded[0:8, :] = jnp.zeros((8, width), F32)
        padded[padded.shape[0] - 8 :, :] = jnp.zeros((8, width), F32)
        for part in range(frames // rows):
            cut = slice(part * rows, (part + 1) * rows)
            here = lax.broadcasted_iota(jnp.int32, (rows, 1), 0) + part * rows < lengths[0]
            extra = mean_grad + var_grad * (convolved[cut, :] - mean)
            padded[8 + part * rows : 8 + (part + 1) * rows, :] = direct[cut, :] + jnp.where(here, extra, 0.0)

    valid = valid_rows(lengths, step, rows)
    passed = gated[...]
    base = pl.multiple_of(step * rows, 8)
    grad = jnp.zeros((rows, width), F32)
    window = padded[pl.ds(base, rows + 16), :]
    tap_sums = []
    for tap in range(9):
        shifted = window[12 - tap : 12 - tap + rows, :]
        grad = grad + shifted * row_of(table, TAPS + tap)
        tap_sums.append(column_sum(shifted * passed))
    grad = grad * valid
    opened = gate[...]
    left = (grad * opened).astype(LOW)
    right = (grad * passed * (1.0 - opened)).astype(LOW)
    doubled_low[:, :width] = left
    doubled_low[:, width:] = right
    unit, scale = normalize(x2[...])
    back = nt(left, point[:, :width]) + nt(right, point[:, width:])
    g2 = stream[...] + norm_backward(back, row_of(table, MIXING_GAIN), unit, scale)
    stream_out[...] = g2
    low = g2.astype(LOW)
    out_low[...] = low
    gather_rows(
        sums,
        0,
        [
            column_sum(back * unit),
            column_sum(back),
            column_sum(left.astype(F32)),
            column_sum(right.astype(F32)),
        ]
        + tap_sums
        + [column_sum(low.astype(F32))],
    )
    grad_mixed = nt(low, output[...]).astype(LOW).astype(F32)
    product = grad_mixed * mixed_wide[...]
    lanes = lane_index(rows)
    for head in range(HEADS):
        pair = product[:, (head // 2) * LANES : (head // 2 + 1) * LANES]
        mine = (lanes < HEAD) if head % 2 == 0 else (lanes >= HEAD)
        inner = jnp.sum(jnp.where(mine, pair, 0.0), axis=-1, keepdims=True)
        high, middle, rest = split_three(-inner)
        marked = jnp.where(lanes < HEAD, head_lanes(grad_mixed, head), 0.0)
        marked = jnp.where(lanes == HEAD + 1, high, marked)
        marked = jnp.where(lanes == HEAD + 2, middle, marked)
        grads[head, :, :] = jnp.where(lanes == HEAD + 3, rest, marked).astype(LOW)


def attend_back_kernel(queries, keys, values, grads, query_grad, key_grad, value_grad):
    frames = queries.shape[1]
    chunk = 256
    turned = []
    for side in range(2):
        query = queries[side, :, :]
        grad = grads[side, :, :]
        total = jnp.zeros((LANES, frames), F32)
        key_parts = []
        value_parts = []
        for part in range(frames // chunk):
            cut = slice(part * chunk, (part + 1) * chunk)
            key = keys[side, cut, :]
            softened = jnp.exp(nt(key, query))
            value_parts.append(nn(softened.astype(LOW), grad))
            low = (softened * nt(values[side, cut, :], grad)).astype(LOW)
            key_parts.append(nn(low, query))
            total = total + tn(key, low)
        turned.append((total[0:HEAD, :], key_parts, value_parts))
    both = jnp.concatenate([turned[0][0], turned[1][0]], axis=0) * HEAD ** (-0.5)
    query_grad[...] = both.T.astype(LOW)
    for part in range(frames // chunk):
        cut = slice(part * chunk, (part + 1) * chunk)
        key_grad[cut, :] = join_pair(turned[0][1][part], turned[1][1][part]).astype(LOW)
        value_grad[cut, :] = join_pair(turned[0][2][part], turned[1][2][part]).astype(LOW)


def first_back_kernel(
    query_grad, key_grad, value_grad, x1, stream, slope, table, query, key, value, reducer,
    stream_out, half_low, inner_low, sums, wide_sums,
):
    step = pl.program_id(0)

    @pl.when(step == 0)
    def _():
        sums[...] = jnp.zeros_like(sums)
        wide_sums[...] = jnp.zeros_like(wide_sums)

    unit, scale = normalize(x1[...])
    back = nt(query_grad[...], query[...]) + nt(key_grad[...], key[...]) + nt(value_grad[...], value[...])
    g1 = stream[...] + norm_backward(back, row_of(table, ATTEND_GAIN), unit, scale)
    stream_out[...] = g1
    low = (0.5 * g1).astype(LOW)
    half_low[...] = low
    gather_rows(
        sums,
        0,
        [
            column_sum(back * unit),
            column_sum(back),
            column_sum(query_grad[...].astype(F32)),
            column_sum(value_grad[...].astype(F32)),
            column_sum(low.astype(F32)),
        ],
    )
    width = 512
    for part in range(slope.shape[1] // width):
        cut = slice(part * width, (part + 1) * width)
        inner = (nt(low, reducer[cut, :]) * slope[:, cut].astype(F32)).astype(LOW)
        inner_low[:, cut] = inner
        wide_sums[part : part + 1, :] += column_sum(inner.astype(F32))


def input_kernel(inner_low, x, stream, table, expand, input_gradient, sums):
    step = pl.program_id(0)

    @pl.when(step == 0)
    def _():
        sums[...] = jnp.zeros_like(sums)

    unit, scale = normalize(x[...].astype(F32))
    back = nt(inner_low[...], expand[...])
    gather_rows(sums, 0, [column_sum(back * unit), column_sum(back)])
    g0 = stream[...] + norm_backward(back, row_of(table, GAIN_ONE), unit, scale)
    input_gradient[...] = g0.astype(LOW)


def whole(array):
    return pl.BlockSpec(array.shape, lambda step: (0,) * len(array.shape))


def tiled(array):
    if len(array.shape) == 3:
        return pl.BlockSpec((array.shape[0], TILE, array.shape[2]), lambda step: (0, step, 0))
    return pl.BlockSpec((TILE, array.shape[1]), lambda step: (step, 0))


SCALAR = pl.BlockSpec(memory_space=pltpu.SMEM)


def shaped(dims, dtype):
    return jax.ShapeDtypeStruct(dims, dtype)


def call(kernel, steps, operands, results, scratch=(), flops=0, limit=56):
    arrays = [array for array, spec in operands]
    moved = sum(array.size * array.dtype.itemsize for array in arrays)
    moved += sum(array.size * array.dtype.itemsize for array, spec in results)
    return pl.pallas_call(
        kernel,
        grid=(steps,),
        in_specs=[spec if isinstance(spec, pl.BlockSpec) else spec(array) for array, spec in operands],
        out_specs=[spec if isinstance(spec, pl.BlockSpec) else spec(array) for array, spec in results],
        out_shape=[array for array, spec in results],
        scratch_shapes=list(scratch),
        compiler_params=pltpu.CompilerParams(vmem_limit_bytes=limit << 20),
        cost_estimate=pl.CostEstimate(flops=flops, bytes_accessed=moved, transcendentals=0),
    )(*arrays)


def weight_grads(pairs, steps=4):
    operands = []
    results = []
    flops = 0
    for left, right in pairs:
        rows = left.shape[1] // steps
        operands.append((left, pl.BlockSpec((left.shape[0], rows), lambda step: (0, step))))
        operands.append((right, whole))
        results.append(
            (
                shaped((left.shape[1], right.shape[1]), F32),
                pl.BlockSpec((rows, right.shape[1]), lambda step: (step, 0)),
            )
        )
        flops += 2 * left.shape[0] * left.shape[1] * right.shape[1]
    return call(weight_kernel(len(pairs)), steps, operands, results, flops=flops)


def bits_of(axis):
    return lax.axis_size(axis).bit_length() - 1


def exchange(values, axis, bit):
    count = lax.axis_size(axis)
    return lax.ppermute(values, axis, [(at, at ^ (1 << bit)) for at in range(count)])


def own_bit(axis, bit):
    return (lax.axis_index(axis) >> bit) & 1


def every_bit():
    return [(axis, bit) for axis in AXES for bit in range(bits_of(axis))]


def halve(values, axis, bit):
    half = values.shape[0] // 2
    mine = own_bit(axis, bit)
    arrived = exchange(lax.dynamic_slice_in_dim(values, (1 - mine) * half, half), axis, bit)
    return lax.dynamic_slice_in_dim(values, mine * half, half) + arrived


def double(values, axis, bit):
    arrived = exchange(values, axis, bit)
    upper = own_bit(axis, bit) == 1
    return jnp.concatenate([jnp.where(upper, arrived, values), jnp.where(upper, values, arrived)])


def part_orders():
    pair = every_bit()[0]
    rest_dp = [step for step in every_bit()[1:] if step[0] == "dp"]
    rest_stream = [step for step in every_bit() if step[0] == "stream"]
    return [
        [pair] + rest_dp + rest_stream,
        [pair] + rest_dp[::-1] + rest_stream,
        [pair] + rest_stream + rest_dp,
    ]


def sum_parts(parts):
    orders = part_orders()
    steps = len(orders[0])
    for at in range(steps):
        parts = [halve(part, *orders[which % 3][at]) for which, part in enumerate(parts)]
    for at in reversed(range(steps)):
        parts = [double(part, *orders[which % 3][at]) for which, part in enumerate(parts)]
    return parts


def sum_small(values):
    for axis, bit in every_bit():
        values = values + exchange(values, axis, bit)
    return values


def join_moments(packed):
    for axis, bit in every_bit():
        other = exchange(packed, axis, bit)
        both = packed + other
        gap = packed[1] / packed[0] - other[1] / other[0]
        extra = gap * gap * (packed[0] * other[0] / both[0])
        packed = jnp.concatenate([both[0:2], both[2:3] + extra[None], both[3:]])
    return packed


def body(
    inputs, lengths, cotangent,
    gain_one, shift_one, expand_one, lift_one, reduce_one, offset_one,
    attend_gain, attend_shift, query_proj, query_bias, key_proj, value_proj, value_bias, output_proj, output_bias,
    mixing_gain, mixing_shift, point_first, first_bias, depth_kernel, batch_gain, batch_shift, point_second, second_bias,
    gain_two, shift_two, expand_two, lift_two, reduce_two, offset_two, final_gain, final_shift,
):
    utterances, frames, width = inputs.shape
    hidden = expand_one.shape[1]
    steps = frames // TILE
    x = inputs.reshape(frames, width)
    cotangent_rows = cotangent.reshape(frames, width)
    table = jnp.concatenate(
        [
            vector.reshape(-1, width)
            for vector in (
                gain_one, shift_one, offset_one, attend_gain, attend_shift, query_bias, value_bias, output_bias,
                mixing_gain, mixing_shift, batch_gain, batch_shift, second_bias, gain_two, shift_two, offset_two,
                final_gain, final_shift, first_bias, depth_kernel,
            )
        ]
    ).astype(F32)
    table = jnp.pad(table, ((0, 32 - table.shape[0]), (0, 0)))
    lift_first = lift_one.astype(F32).reshape(1, hidden)
    lift_second = lift_two.astype(F32).reshape(1, hidden)
    rows_low = shaped((frames, width), LOW)
    rows_full = shaped((frames, width), F32)
    hidden_low = shaped((frames, hidden), LOW)
    heads_low = shaped((HEADS, frames, LANES), LOW)

    def small(rows):
        return (shaped((rows, width), F32), whole)

    normed_a, acted_a, slope_a, x1, normed_b, queries, keys, values, sums_a = call(
        front_kernel,
        steps,
        [
            (lengths, SCALAR), (x, tiled), (table, whole), (lift_first, whole), (expand_one, whole),
            (reduce_one, whole), (query_proj, whole), (key_proj, whole), (value_proj, whole),
        ],
        [
            (rows_low, tiled), (hidden_low, tiled), (hidden_low, tiled), (rows_full, tiled), (rows_low, tiled),
            (heads_low, tiled), (heads_low, tiled), (heads_low, tiled), small(8),
        ],
        flops=2 * frames * width * (2 * hidden + 3 * width),
    )
    again, mixed_wide, mixed, x2, normed_c, gated, gate_c, convolved, moments, sums_b = call(
        attend_kernel,
        steps,
        [
            (lengths, SCALAR), (queries, tiled), (keys, whole), (values, whole), (x1, tiled), (table, whole),
            (output_proj, whole), (point_first, whole),
        ],
        [
            (heads_low, tiled), (rows_full, tiled), (rows_low, tiled), (rows_full, tiled), (rows_low, tiled),
            (rows_full, tiled), (rows_full, tiled), (rows_full, whole), small(8), small(8),
        ],
        scratch=[pltpu.VMEM((frames + 16, width), F32)],
        flops=8 * frames * frames * width,
    )
    moments = join_moments(moments)
    (
        block_output, acted_c, low_c, acted_d, half_d, normed_d, inner_d, g3, direct, sums_c, lift_two_sums,
    ) = call(
        rear_kernel,
        steps,
        [
            (lengths, SCALAR), (convolved, tiled), (x2, tiled), (cotangent_rows, tiled), (moments, whole),
            (table, whole), (lift_second, whole), (point_second, whole), (expand_two, whole), (reduce_two, whole),
        ],
        [
            (rows_low, tiled), (rows_low, tiled), (rows_low, tiled), (hidden_low, tiled), (rows_low, tiled),
            (rows_low, tiled), (hidden_low, tiled), (rows_full, tiled), (rows_full, tiled), small(16), small(8),
        ],
        flops=2 * frames * width * (4 * hidden + 2 * width),
    )
    batch_sums = sum_small(sums_c[0:8])
    grad_reduce_two, grad_expand_two, grad_second = weight_grads(
        [(acted_d, half_d), (normed_d, inner_d), (acted_c, low_c)]
    )
    second_large = lax.psum((grad_expand_two, grad_reduce_two), AXES)
    doubled_low, g2, out_low, mixed_grads, sums_d = call(
        mixing_kernel,
        steps,
        [
            (lengths, SCALAR), (moments, whole), (batch_sums, whole), (direct, whole), (convolved, whole),
            (gated, tiled), (gate_c, tiled), (x2, tiled), (g3, tiled), (mixed_wide, tiled), (table, whole),
            (point_first, whole), (output_proj, whole),
        ],
        [
            (shaped((frames, 2 * width), LOW), tiled), (rows_full, tiled), (rows_low, tiled), (heads_low, tiled),
            small(16),
        ],
        scratch=[pltpu.VMEM((frames + 16, width), F32)],
        flops=2 * frames * width * 3 * width,
    )
    grad_point_first, grad_output = weight_grads([(normed_c, doubled_low), (mixed, out_low)])
    pair_block = pl.BlockSpec((2, frames, LANES), lambda step: (step, 0, 0))
    lane_block = pl.BlockSpec((frames, LANES), lambda step: (0, step))
    query_grad, key_grad, value_grad = call(
        attend_back_kernel,
        HEADS // 2,
        [(again, pair_block), (keys, pair_block), (values, pair_block), (mixed_grads, pair_block)],
        [(rows_low, lane_block), (rows_low, lane_block), (rows_low, lane_block)],
        flops=20 * frames * frames * width,
    )
    g1, half_a, inner_a, sums_e, lift_one_sums = call(
        first_back_kernel,
        steps,
        [
            (query_grad, tiled), (key_grad, tiled), (value_grad, tiled), (x1, tiled), (g2, tiled), (slope_a, tiled),
            (table, whole), (query_proj, whole), (key_proj, whole), (value_proj, whole), (reduce_one, whole),
        ],
        [(rows_full, tiled), (rows_low, tiled), (hidden_low, tiled), small(8), small(8)],
        flops=2 * frames * width * (hidden + 3 * width),
    )
    grad_query, grad_key, grad_value = weight_grads(
        [(normed_b, query_grad), (normed_b, key_grad), (normed_b, value_grad)]
    )
    grad_reduce_one, grad_expand_one = weight_grads([(acted_a, half_a), (normed_a, inner_a)])
    input_gradient, sums_f = call(
        input_kernel,
        steps,
        [(inner_a, tiled), (x, tiled), (g1, tiled), (table, whole), (expand_one, whole)],
        [(rows_low, tiled), small(8)],
        flops=2 * frames * width * hidden,
    )
    large = jnp.concatenate(
        [
            grad_point_first[:, :width], grad_point_first[:, width:], grad_second, grad_query, grad_key, grad_value,
            grad_output, sums_a, sums_b, sums_c, lift_two_sums, sums_d, jnp.zeros((72, width), F32),
        ]
    )
    cut = 1408
    middle = jnp.concatenate(sum_parts([large[:cut], large[cut : 2 * cut], large[2 * cut :]]))
    first_reduce, first_expand = sum_parts([grad_reduce_one, grad_expand_one])
    late = sum_small(jnp.concatenate([sums_e, lift_one_sums, sums_f]))
    tail = middle[7 * width :]
    total_a, total_b, total_c, total_lift, total_d = (
        tail[0:8], tail[8:16], tail[16:32], tail[32:40], tail[40:56],
    )
    total_e, total_lift_one, total_f = late[0:8], late[8:16], late[16:24]
    squares = jnp.sum(
        jnp.stack(
            [
                total_a[0], total_b[0], total_c[8], total_c[10], total_a[1], total_b[1], total_c[9], total_c[11],
            ]
        ),
        axis=1,
    )
    rms_stats = jnp.sqrt(squares / (moments[0, 0] * width))

    def block(at):
        return middle[at * width : (at + 1) * width]

    return (
        block_output.reshape(inputs.shape),
        input_gradient.reshape(inputs.shape),
        total_f[0],
        total_f[1],
        first_expand,
        total_lift_one[0 : hidden // width].reshape(-1),
        first_reduce,
        total_e[4],
        total_e[0],
        total_e[1],
        block(3),
        total_e[2],
        block(4),
        block(5),
        total_e[3],
        block(6),
        total_d[13],
        total_d[0],
        total_d[1],
        jnp.concatenate([block(0), block(1)], axis=1),
        total_d[2:4].reshape(-1),
        total_d[4:13],
        batch_sums[1],
        batch_sums[0],
        block(2),
        total_c[2],
        total_c[3],
        total_c[4],
        second_large[0],
        total_lift[0 : hidden // width].reshape(-1),
        second_large[1],
        total_c[5],
        total_c[6],
        total_c[7],
        rms_stats,
    )


def solution(mesh):
    rows = P(AXES, None, None)
    return jax.shard_map(
        body,
        mesh=mesh,
        in_specs=(rows, P(AXES), rows) + (P(),) * 32,
        out_specs=(rows, rows) + (P(),) * 33,
        check_vma=False,
    )
```

time: 1150 us -> 528 us (0.46); the launches traced: 1130 us -> 524 us
  local copies, waits for them, and re-layouts: 338 us -> 38.2 us
  waiting for transfers between devices: 374 us -> 201 us
  Pallas kernels: 0 us -> 165 us
  matrix products: 159 us -> 0 us
  blocking collectives: 123 us -> 0 us
  other arithmetic: 119 us -> 32.3 us
  starting transfers between devices: 0.04 us -> 70.7 us
    psum x1, waiting for transfers between devices: 374 us -> 0.01 us  [body(): second_large = lax.psum((grad_expand_two, grad_reduce_two), AXES)]
    concatenate x1 -> x3, local copies, waits for them, and re-layouts: 209 us -> 1.64 us  [the longest x1 0.91 us: body(): jnp.concatenate([vector.reshape(-1, width) for vector in (gain_one, shift...]
    ppermute x0 -> x65, waiting for transfers between devices: none -> 201 us  [exchange(): lax.ppermute(values, axis, [(at, at ^ 1 << bit) for at in range(count)])]
    pallas_call x0 -> x11, Pallas kernels: none -> 165 us  [call(): pl.pallas_call(kernel, grid=(steps,), in_specs=[spec if isinstance(spec,...]
    dot_general x44 -> x0, matrix products: 159 us -> none  [the longest x10 29.5 us: row_contract(): lax.dot_general(operand_one, operand_two, (((0,), (0,)), ((), ())), prefe...]
    psum x3 -> x0, blocking collectives: 123 us -> none  [the longest x1 42.2 us: body(): lax.psum((frames_here, column_sum(convolved * validity_rows)), ('dp', 'st...]
    ppermute x0 -> x65, starting transfers between devices: none -> 70.7 us  [exchange(): lax.ppermute(values, axis, [(at, at ^ 1 << bit) for at in range(count)])]
    reduce_sum x28 -> x1, other arithmetic: 57.9 us -> 0.63 us  [body(): jnp.sum(jnp.stack([total_a[0], total_b[0], total_c[8], total_c[10], total...]
  transfers between devices with their start and end apart: 1 -> 66, of which waited for: 1 -> 41; matrix products, arithmetic and copies ran while one was open for 0% -> 8% of each run, Pallas kernels for 0% -> 18%
where the time goes in v2:
time: 528 us; the launch traced here: 524 us
  waiting for transfers between devices  201 us (38%)
  Pallas kernels  165 us (31%)
  starting transfers between devices  70.7 us (13%)
  local copies, waits for them, and re-layouts  38.2 us (7%)
  other arithmetic  32.3 us (6%)
  between operations  16.8 us (3%)
    ppermute x65, waiting for transfers between devices, exchange(): lax.ppermute(values, axis, [(at, at ^ 1 << bit) for at in range(count)])  201 us
    pallas_call x11, Pallas kernels, call(): pl.pallas_call(kernel, grid=(steps,), in_specs=[spec if isinstance(spec,...  165 us
    ppermute x65, starting transfers between devices, exchange(): lax.ppermute(values, axis, [(at, at ^ 1 << bit) for at in range(count)])  70.7 us
    unnamed x57, local copies, waits for them, and re-layouts  16.5 us
    reshape x19, local copies, waits for them, and re-layouts, body(): vector.reshape(-1, width)  13 us
  transfers between devices with their start and end apart: 66, of which 41 were waited for; matrix products, arithmetic and copies ran while one was open for 8% of the time, Pallas kernels for 18%

profile of v2, /device:TPU:0, one launch (start us, length us, event | category | flops | bytes accessed | tf_op | source)
XLA Modules:
  0.0 524.0 jit_solution(1290846507436418918)
XLA Ops:
  23.7 17.1 %shard_map.602 = (bf16[1024,512]{1,0:T(8,128)(2,1)}, bf16[1024,2048]{1,0:T(8,128)(2,1)}, bf16[1024,2048]{1,0:T(8,128)(2,1)}, f32[1024,512]{1,0:T(8,128)}, bf16[1...) custom-call(s32[1]{0:T(128)S(6)} %copy.84.lengths, ...), custom_call_target="tpu_custom_call" | custom-call | flops 5905580032 | bytes 25780228 | tf_op jit(solution)/shard_map/pallas_call | solution.py:493
  40.8 30.7 %shard_map.603 = (bf16[8,1024,128]{2,1,0:T(8,128)(2,1)}, f32[1024,512]{1,0:T(8,128)}, bf16[1024,512]{1,0:T(8,128)(2,1)}, f32[1024,512]{1,0:T(8,128)}, bf16[1024,...) custom-call(s32[1]{0:T(128)S(6)} %copy.84.lengths, ...), custom_call_target="tpu_custom_call" | custom-call | flops 4294967296 | bytes 24739844 | tf_op jit(solution)/shard_map/pallas_call | solution.py:493
  74.7 2.9 collective-permute-start.1
  77.6 1.7 collective-permute-done.1
  79.4 2.1 collective-permute-start.2
  81.5 1.7 collective-permute-done.2
  83.3 2.1 collective-permute-start.3
  85.4 1.7 collective-permute-done.3
  87.2 3.1 collective-permute-start.4
  92.7 23.7 %shard_map.604 = (bf16[1024,512]{1,0:T(8,128)(2,1)}, bf16[1024,512]{1,0:T(8,128)(2,1)}, bf16[1024,512]{1,0:T(8,128)(2,1)}, bf16[1024,2048]{1,0:T(8,128)(2,1)}, b...) custom-call(s32[1]{0:T(128)S(6)} %copy.84.lengths, ...), custom_call_target="tpu_custom_call" | custom-call | flops 9663676416 | bytes 27926532 | tf_op jit(solution)/shard_map/pallas_call | solution.py:493
  119.0 1.8 collective-permute-start.6
  120.9 1.9 collective-permute-done.6
  122.8 1.9 collective-permute-start.7
  124.7 1.9 collective-permute-done.7
  126.5 1.9 collective-permute-start.8
  128.4 1.8 collective-permute-done.8
  130.3 2.9 collective-permute-start.9
  133.2 10.4 %shard_map.610 = (f32[2048,512]{1,0:T(8,128)}, f32[512,2048]{1,0:T(8,128)}, f32[512,512]{1,0:T(8,128)}) custom-call(bf16[1024,2048]{1,0:T(8,128)(2,1)} %get-tuple-element.122.refs_0_, bf16[1024,512]{1,0:T(8,128)(2,1)} %get-tuple-element.123.refs_1_, bf16[1024,512]{1,0:T(8,128)(2,1)} %get-tuple-element.124.refs_2_, ...), custom_call_target="tpu_custom_call" | custom-call | flops 4831838208 | bytes 22020096 | tf_op jit(solution)/shard_map/pallas_call | solution.py:493
  145.4 18.4 %shard_map.605 = (bf16[1024,1024]{1,0:T(8,128)(2,1)}, f32[1024,512]{1,0:T(8,128)}, bf16[1024,512]{1,0:T(8,128)(2,1)}, bf16[8,1024,128]{2,1,0:T(8,128)(2,1)}, f32[16,512]{1,0:T(8,128)}) custom-call(s32[1]{0:T(128)S(6)} %copy.84.lengths, f32[8,512]{1,0:T(8,128)} %pad_maximum_fusion.36.moments, f32[8,512]{1,0:T(8,128)} %add.293.batch_sums, ...), custom_call_target="tpu_custom_call" | custom-call | flops 1610612736 | bytes 23724036 | tf_op jit(solution)/shard_map/pallas_call | solution.py:493
  163.8 23.7 %shard_map.606 = (bf16[1024,512]{1,0:T(8,128)(2,1)}, bf16[1024,512]{1,0:T(8,128)(2,1)}, bf16[1024,512]{1,0:T(8,128)(2,1)}) custom-call(bf16[8,1024,128]{2,1,0:T(8,128)(2,1)} %get-tuple-element.98.queries, bf16[8,1024,128]{2,1,0:T(8,128)(2,1)} %get-tuple-element.91.keys, bf16[8,1024,128]{2,1,0:T(8,128)(2,1)} %get-tuple-element.92.values, ...), custom_call_target="tpu_custom_call" | custom-call | flops 10737418240 | bytes 11534336 | tf_op jit(solution)/shard_map/pallas_call | solution.py:493
  187.5 6.2 %shard_map.611 = (f32[512,512]{1,0:T(8,128)}, f32[512,512]{1,0:T(8,128)}, f32[512,512]{1,0:T(8,128)}) custom-call(bf16[1024,512]{1,0:T(8,128)(2,1)} %get-tuple-element.129.refs_0_.refs_2_.refs_4_, bf16[1024,512]{1,0:T(8,128)(2,1)} %get-tuple-element.106.query_grad.refs_1_, bf16[1024,512]{1,0:T(8,128)(2,1)} %get-tuple-element.129.refs_0_.refs_2_.refs_4_, ...), custom_call_target="tpu_custom_call" | custom-call | flops 1610612736 | bytes 9437184 | tf_op jit(solution)/shard_map/pallas_call | solution.py:493
  195.0 5.9 %shard_map.612 = (f32[512,1024]{1,0:T(8,128)}, f32[512,512]{1,0:T(8,128)}) custom-call(bf16[1024,512]{1,0:T(8,128)(2,1)} %get-tuple-element.133.refs_0_, bf16[1024,1024]{1,0:T(8,128)(2,1)} %get-tuple-element.134.refs_1_, bf16[1024,512]{1,0:T(8,128)(2,1)} %get-tuple-element.135.refs_2_, bf16[1024,512]{1,0:T(8,128)(2,1)} %get-tuple-element.136.refs_3_), custom_call_target="tpu_custom_call" | custom-call | flops 1610612736 | bytes 8388608 | tf_op jit(solution)/shard_map/pallas_call | solution.py:493
  202.7 11.3 %shard_map.607 = (f32[1024,512]{1,0:T(8,128)}, bf16[1024,512]{1,0:T(8,128)(2,1)}, bf16[1024,2048]{1,0:T(8,128)(2,1)}, f32[8,512]{1,0:T(8,128)}, f32[8,512]{1,0:T(8,128)}) custom-call(bf16[1024,512]{1,0:T(8,128)(2,1)} %get-tuple-element.106.query_grad.refs_1_, bf16[1024,512]{1,0:T(8,128)(2,1)} %get-tuple-element.107.key_grad.refs_3_, ...), custom_call_target="tpu_custom_call" | custom-call | flops 3758096384 | bytes 22642688 | tf_op jit(solution)/shard_map/pallas_call | solution.py:493
  215.5 7.4 %shard_map.608 = (bf16[1024,512]{1,0:T(8,128)(2,1)}, f32[8,512]{1,0:T(8,128)}) custom-call(bf16[1024,2048]{1,0:T(8,128)(2,1)} %get-tuple-element.111.inner_low.refs_3_, bf16[1024,512]{1,0:T(8,128)(2,1)} %bitcast.35, f32[1024,512]{1,0:T(8,128)} %get-tuple-element.112.stream, f32[32,512]{1,0:T(8,128)} %pad_convert_fusion.table, bf16[512,2048]{1,0:T(8,128)(2,1)} %expand.5), custom_call_target="tpu_custom_call" | custom-call | flops 2147483648 | bytes 10567680 | tf_op jit(solution)/shard_map/pallas_call | solution.py:493
  224.1 10.2 %shard_map.609 = (f32[2048,512]{1,0:T(8,128)}, f32[512,2048]{1,0:T(8,128)}) custom-call(bf16[1024,2048]{1,0:T(8,128)(2,1)} %get-tuple-element.117.refs_0_, bf16[1024,512]{1,0:T(8,128)(2,1)} %get-tuple-element.118.refs_1_, bf16[1024,512]{1,0:T(8,128)(2,1)} %get-tuple-element.119.refs_2_, bf16[1024,2048]{1,0:T(8,128)(2,1)} %get-tuple-element.111.inner_low.refs_3_), custom_call_target="tpu_custom_call" | custom-call | flops 4294967296 | bytes 18874368 | tf_op jit(solution)/shard_map/pallas_call | solution.py:493
  240.3 2.8 collective-permute-done.11
  249.2 10.3 %collective-permute-done.13 = f32[24,512]{1,0:T(8,128)S(1)} collective-permute-done((f32[24,512]{1,0:T(8,128)S(1)}, f32[24,512]{1,0:T(8,128)S(1)}, u32[]{:S(2)}, u32[]{:S(2)}) %collective-permute-start.13) | collective-permute-done | bytes 49184 | tf_op jit(solution)/shard_map/ppermute | solution.py:529
  260.0 7.1 %collective-permute-done.14 = f32[24,512]{1,0:T(8,128)S(1)} collective-permute-done((f32[24,512]{1,0:T(8,128)S(1)}, f32[24,512]{1,0:T(8,128)S(1)}, u32[]{:S(2)}, u32[]{:S(2)}) %collective-permute-start.14) | collective-permute-done | bytes 49184 | tf_op jit(solution)/shard_map/ppermute | solution.py:529
  268.5 14.8 %collective-permute-done.47 = f32[112,512]{1,0:T(8,128)S(1)} collective-permute-done((f32[112,512]{1,0:T(8,128)S(1)}, f32[112,512]{1,0:T(8,128)S(1)}, u32[]{:S(2)}, u32[]{:S(2)}) %collective-permute-start.47) | collective-permute-done | bytes 229408 | tf_op jit(solution)/shard_map/ppermute | solution.py:529
  285.4 4.8 collective-permute-done.48
  290.4 2.1 collective-permute-start.36
  292.4 4.2 collective-permute-done.49
  297.1 26.3 %collective-permute-done.50 = f32[28,512]{1,0:T(8,128)S(1)} collective-permute-done((f32[28,512]{1,0:T(8,128)S(1)}, f32[28,512]{1,0:T(8,128)S(1)}, u32[]{:S(2)}, u32[]{:S(2)}) %collective-permute-start.50) | collective-permute-done | bytes 57376 | tf_op jit(solution)/shard_map/ppermute | solution.py:529
  325.6 3.9 collective-permute-done.51
  329.5 1.9 collective-permute-start.52
  332.0 1.9 collective-permute-start.26
  335.8 9.1 %collective-permute-done.56 = f32[352,512]{1,0:T(8,128)S(1)} collective-permute-done((f32[352,512]{1,0:T(8,128)S(1)}, f32[352,512]{1,0:T(8,128)S(1)}, u32[]{:S(2)}, u32[]{:S(2)}) %collective-permute-start.56) | collective-permute-done | bytes 720928 | tf_op jit(solution)/shard_map/ppermute | solution.py:529
  345.5 1.9 collective-permute-start.53
  347.5 26.2 %collective-permute-done.37 = f32[176,512]{1,0:T(8,128)S(1)} collective-permute-done((f32[176,512]{1,0:T(8,128)S(1)}, f32[176,512]{1,0:T(8,128)S(1)}, u32[]{:S(2)}, u32[]{:S(2)}) %collective-permute-start.37) | collective-permute-done | bytes 360480 | tf_op jit(solution)/shard_map/ppermute | solution.py:529
  376.0 5.9 %collective-permute-done.38 = f32[88,512]{1,0:T(8,128)S(1)} collective-permute-done((f32[88,512]{1,0:T(8,128)S(1)}, f32[88,512]{1,0:T(8,128)S(1)}, u32[]{:S(2)}, u32[]{:S(2)}) %collective-permute-start.38) | collective-permute-done | bytes 180256 | tf_op jit(solution)/shard_map/ppermute | solution.py:529
  383.9 2.8 collective-permute-start.59
  386.7 5.3 %collective-permute-done.39 = f32[44,512]{1,0:T(8,128)S(1)} collective-permute-done((f32[44,512]{1,0:T(8,128)S(1)}, f32[44,512]{1,0:T(8,128)S(1)}, u32[]{:S(2)}, u32[]{:S(2)}) %collective-permute-start.39) | collective-permute-done | bytes 90144 | tf_op jit(solution)/shard_map/ppermute | solution.py:529
  392.1 2.0 collective-permute-done.59
  395.1 4.3 collective-permute-done.40
  402.9 2.2 collective-permute-done.41
  405.0 1.9 collective-permute-done.61
  411.9 6.6 %collective-permute-done.62 = f32[176,512]{1,0:T(8,128)S(1)} collective-permute-done((f32[176,512]{1,0:T(8,128)S(1)}, f32[176,512]{1,0:T(8,128)S(1)}, u32[]{:S(2)}, u32[]{:S(2)}) %collective-permute-start.62) | collective-permute-done | bytes 360480 | tf_op jit(solution)/shard_map/ppermute | solution.py:529
  423.9 5.9 %collective-permute-done.27 = f32[256,512]{1,0:T(8,128)S(1)} collective-permute-done((f32[256,512]{1,0:T(8,128)S(1)}, f32[256,512]{1,0:T(8,128)S(1)}, u32[]{:S(2)}, u32[]{:S(2)}) %collective-permute-start.27) | collective-permute-done | bytes 524320 | tf_op jit(solution)/shard_map/ppermute | solution.py:529
  432.1 6.2 %collective-permute-done.28 = f32[128,512]{1,0:T(8,128)S(1)} collective-permute-done((f32[128,512]{1,0:T(8,128)S(1)}, f32[128,512]{1,0:T(8,128)S(1)}, u32[]{:S(2)}, u32[]{:S(2)}) %collective-permute-start.28) | collective-permute-done | bytes 262176 | tf_op jit(solution)/shard_map/ppermute | solution.py:529
  440.0 5.3 %collective-permute-done.18 = f32[32,2048]{1,0:T(8,128)S(1)} collective-permute-done((f32[32,2048]{1,0:T(8,128)S(1)}, f32[32,2048]{1,0:T(8,128)S(1)}, u32[]{:S(2)}, u32[]{:S(2)}) %collective-permute-start.18) | collective-permute-done | bytes 262176 | tf_op jit(solution)/shard_map/ppermute | solution.py:529
  446.5 2.5 collective-permute-start.30
  449.0 3.7 collective-permute-done.19
  453.9 1.7 collective-permute-done.30
  455.6 1.8 collective-permute-start.31
  457.4 2.8 collective-permute-done.20
  460.4 2.0 collective-permute-done.31
  471.4 7.7 %collective-permute-done.32 = f32[256,512]{1,0:T(8,128)} collective-permute-done((f32[256,512]{1,0:T(8,128)}, f32[256,512]{1,0:T(8,128)}, u32[]{:S(2)}, u32[]{:S(2)}) %collective-permute-start.32) | collective-permute-done | bytes 524320 | tf_op jit(solution)/shard_map/ppermute | solution.py:529
  487.0 8.3 %collective-permute-done.33 = f32[512,512]{1,0:T(8,128)S(1)} collective-permute-done((f32[512,512]{1,0:T(8,128)S(1)}, f32[512,512]{1,0:T(8,128)S(1)}, u32[]{:S(2)}, u32[]{:S(2)}) %collective-permute-start.33) | collective-permute-done | bytes 1048608 | tf_op jit(solution)/shard_map/ppermute | solution.py:529
  496.0 1.7 collective-permute-done.23
  501.6 2.4 pad_maximum_fusion.12
  504.5 2.5 pad_maximum_fusion.1
  507.5 2.5 pad_maximum_fusion
  510.1 4.8 copy.85
  514.9 2.0 copy.86
  (308 shorter events, 100.6 us)
Async XLA Ops:
  7.2 502.8 %all-reduce.4.cloned.1.call-start = ((), (), s32[]{:S(2)}) async-start(), calls=%async_computation | async-start | bytes 16777216 | tf_op jit(solution)/shard_map/psum | solution.py:670
  74.7 4.6 collective-permute-start.1
  79.4 3.8 collective-permute-start.2
  83.3 3.8 collective-permute-start.3
  87.2 4.8 collective-permute-start.4
  119.0 3.7 collective-permute-start.6
  122.8 3.7 collective-permute-start.7
  126.5 3.7 collective-permute-start.8
  130.3 14.5 %collective-permute-start.9 = (f32[8,512]{1,0:T(8,128)S(1)}, f32[8,512]{1,0:T(8,128)S(1)}, u32[]{:S(2)}, u32[]{:S(2)}) collective-permute-start(f32[8,512]{1,0:T(8,128)S(1)} %add.292), channel_id=1, source_target_pairs={{0,2},{1,3},{2,0},{3,1},{4,6},{5,7},{6,4},{7,5},{8,10},{9,11},{10,... | collective-permute-start | bytes 49160 | tf_op jit(solution)/shard_map/ppermute | solution.py:529
  202.6 42.1 %collective-permute-start.45 = (f32[448,512]{1,0:T(8,128)S(1)}, f32[448,512]{1,0:T(8,128)S(1)}, u32[]{:S(2)}, u32[]{:S(2)}) collective-permute-start(f32[448,512]{1,0:T(8,128)S(1)} %constant_dynamic-slice_fusion.9), channel_id=1, source_target_pairs={{0,4},{4,0},{8,12},{12,8},{16,20},{20,16},{24,28},{28,24},{1,5},{5... | collective-permute-start | bytes 2752520 | tf_op jit(solution)/shard_map/ppermute | solution.py:529
  223.6 14.9 %collective-permute-start.10 = (f32[24,512]{1,0:T(8,128)S(1)}, f32[24,512]{1,0:T(8,128)S(1)}, u32[]{:S(2)}, u32[]{:S(2)}) collective-permute-start(f32[24,512]{1,0:T(8,128)S(1)} %constant_dynamic-update-slice_fusion), channel_id=1, source_target_pairs={{0,4},{4,0},{8,12},{12,8},{16,20},{20,16},{24,28},{28,24},{1,5},{5... | collective-permute-start | bytes 147464 | tf_op jit(solution)/shard_map/ppermute | solution.py:529
  238.5 4.6 collective-permute-start.11
  240.3 44.8 %collective-permute-start.35 = (f32[704,512]{1,0:T(8,128)S(1)}, f32[704,512]{1,0:T(8,128)S(1)}, u32[]{:S(2)}, u32[]{:S(2)}) collective-permute-start(f32[704,512]{1,0:T(8,128)S(1)} %constant_dynamic-slice_fusion.14), channel_id=1, source_target_pairs={{0,4},{4,0},{8,12},{12,8},{16,20},{20,16},{24,28},{28,24},{1,5},{5... | collective-permute-start | bytes 4325384 | tf_op jit(solution)/shard_map/ppermute | solution.py:529
  243.1 4.2 collective-permute-start.12
  244.9 22.2 %collective-permute-start.46 = (f32[224,512]{1,0:T(8,128)S(1)}, f32[224,512]{1,0:T(8,128)S(1)}, u32[]{:S(2)}, u32[]{:S(2)}) collective-permute-start(f32[224,512]{1,0:T(8,128)S(1)} %constant_dynamic-slice_fusion.8), channel_id=1, source_target_pairs={{0,1},{1,0},{2,3},{3,2},{4,5},{5,4},{6,7},{7,6},{8,9},{9,8},{10,11... | collective-permute-start | bytes 1376264 | tf_op jit(solution)/shard_map/ppermute | solution.py:529
  246.6 50.1 %collective-permute-start.55 = (f32[704,512]{1,0:T(8,128)S(1)}, f32[704,512]{1,0:T(8,128)S(1)}, u32[]{:S(2)}, u32[]{:S(2)}) collective-permute-start(f32[704,512]{1,0:T(8,128)S(1)} %constant_dynamic-slice_fusion.4), channel_id=1, source_target_pairs={{0,4},{4,0},{8,12},{12,8},{16,20},{20,16},{24,28},{28,24},{1,5},{5... | collective-permute-start | bytes 4325384 | tf_op jit(solution)/shard_map/ppermute | solution.py:529
  247.3 12.1 %collective-permute-start.13 = (f32[24,512]{1,0:T(8,128)S(1)}, f32[24,512]{1,0:T(8,128)S(1)}, u32[]{:S(2)}, u32[]{:S(2)}) collective-permute-start(f32[24,512]{1,0:T(8,128)S(1)} %add.296), channel_id=1, source_target_pairs={{0,1},{1,0},{2,3},{3,2},{4,5},{5,4},{6,7},{7,6},{8,9},{9,8},{10,11... | collective-permute-start | bytes 147464 | tf_op jit(solution)/shard_map/ppermute | solution.py:529
  249.1 82.3 %collective-permute-start.25 = (f32[1024,512]{1,0:T(8,128)S(1)}, f32[1024,512]{1,0:T(8,128)S(1)}, u32[]{:S(2)}, u32[]{:S(2)}) collective-permute-start(f32[1024,512]{1,0:T(8,128)S(1)} %constant_dynamic-slice_fusion.19), channel_id=1, source_target_pairs={{0,4},{4,0},{8,12},{12,8},{16,20},{20,16},{24,28},{28,24},{1,5},{5... | collective-permute-start | bytes 6291464 | tf_op jit(solution)/shard_map/ppermute | solution.py:529
  259.4 7.7 %collective-permute-start.14 = (f32[24,512]{1,0:T(8,128)S(1)}, f32[24,512]{1,0:T(8,128)S(1)}, u32[]{:S(2)}, u32[]{:S(2)}) collective-permute-start(f32[24,512]{1,0:T(8,128)S(1)} %add.297), channel_id=1, source_target_pairs={{0,2},{1,3},{2,0},{3,1},{4,6},{5,7},{6,4},{7,5},{8,10},{9,11},{10,... | collective-permute-start | bytes 147464 | tf_op jit(solution)/shard_map/ppermute | solution.py:529
  267.1 66.7 %collective-permute-start.15 = (f32[256,2048]{1,0:T(8,128)S(1)}, f32[256,2048]{1,0:T(8,128)S(1)}, u32[]{:S(2)}, u32[]{:S(2)}) collective-permute-start(f32[256,2048]{1,0:T(8,128)S(1)} %constant_dynamic-slice_fusion.24), channel_id=1, source_target_pairs={{0,4},{4,0},{8,12},{12,8},{16,20},{20,16},{24,28},{28,24},{1,5},{5... | collective-permute-start | bytes 6291464 | tf_op jit(solution)/shard_map/ppermute | solution.py:529
  267.3 16.1 %collective-permute-start.47 = (f32[112,512]{1,0:T(8,128)S(1)}, f32[112,512]{1,0:T(8,128)S(1)}, u32[]{:S(2)}, u32[]{:S(2)}) collective-permute-start(f32[112,512]{1,0:T(8,128)S(1)} %constant_dynamic-slice_fusion.7), channel_id=1, source_target_pairs={{0,2},{1,3},{2,0},{3,1},{4,6},{5,7},{6,4},{7,5},{8,10},{9,11},{10,... | collective-permute-start | bytes 688136 | tf_op jit(solution)/shard_map/ppermute | solution.py:529
  283.4 6.8 %collective-permute-start.48 = (f32[56,512]{1,0:T(8,128)S(1)}, f32[56,512]{1,0:T(8,128)S(1)}, u32[]{:S(2)}, u32[]{:S(2)}) collective-permute-start(f32[56,512]{1,0:T(8,128)S(1)} %constant_dynamic-slice_fusion.6), channel_id=1, source_target_pairs={{0,8},{4,12},{8,0},{12,4},{16,24},{20,28},{24,16},{28,20},{1,9},{5... | collective-permute-start | bytes 344072 | tf_op jit(solution)/shard_map/ppermute | solution.py:529
  290.2 6.4 %collective-permute-start.49 = (f32[28,512]{1,0:T(8,128)S(1)}, f32[28,512]{1,0:T(8,128)S(1)}, u32[]{:S(2)}, u32[]{:S(2)}) collective-permute-start(f32[28,512]{1,0:T(8,128)S(1)} %constant_dynamic-slice_fusion.5), channel_id=1, source_target_pairs={{0,16},{4,20},{8,24},{12,28},{16,0},{20,4},{24,8},{28,12},{1,17},{... | collective-permute-start | bytes 172040 | tf_op jit(solution)/shard_map/ppermute | solution.py:529
  290.4 44.5 %collective-permute-start.36 = (f32[352,512]{1,0:T(8,128)S(1)}, f32[352,512]{1,0:T(8,128)S(1)}, u32[]{:S(2)}, u32[]{:S(2)}) collective-permute-start(f32[352,512]{1,0:T(8,128)S(1)} %constant_dynamic-slice_fusion.13), channel_id=1, source_target_pairs={{0,16},{4,20},{8,24},{12,28},{16,0},{20,4},{24,8},{28,12},{1,17},{... | collective-permute-start | bytes 2162696 | tf_op jit(solution)/shard_map/ppermute | solution.py:529
  296.6 26.7 %collective-permute-start.50 = (f32[28,512]{1,0:T(8,128)S(1)}, f32[28,512]{1,0:T(8,128)S(1)}, u32[]{:S(2)}, u32[]{:S(2)}) collective-permute-start(f32[28,512]{1,0:T(8,128)S(1)} %dynamic-slice_add_fusion.24), channel_id=1, source_target_pairs={{0,16},{4,20},{8,24},{12,28},{16,0},{20,4},{24,8},{28,12},{1,17},{... | collective-permute-start | bytes 172040 | tf_op jit(solution)/shard_map/ppermute | solution.py:529
  323.4 6.1 %collective-permute-start.51 = (f32[56,512]{1,0:T(8,128)S(1)}, f32[56,512]{1,0:T(8,128)S(1)}, u32[]{:S(2)}, u32[]{:S(2)}) collective-permute-start(f32[56,512]{1,0:T(8,128)S(1)} %pad_maximum_fusion.31), channel_id=1, source_target_pairs={{0,8},{4,12},{8,0},{12,4},{16,24},{20,28},{24,16},{28,20},{1,9},{5... | collective-permute-start | bytes 344072 | tf_op jit(solution)/shard_map/ppermute | solution.py:529
  325.0 19.9 %collective-permute-start.56 = (f32[352,512]{1,0:T(8,128)S(1)}, f32[352,512]{1,0:T(8,128)S(1)}, u32[]{:S(2)}, u32[]{:S(2)}) collective-permute-start(f32[352,512]{1,0:T(8,128)S(1)} %constant_dynamic-slice_fusion.3), channel_id=1, source_target_pairs={{0,8},{4,12},{8,0},{12,4},{16,24},{20,28},{24,16},{28,20},{1,9},{5... | collective-permute-start | bytes 2162696 | tf_op jit(solution)/shard_map/ppermute | solution.py:529
  329.5 15.9 %collective-permute-start.52 = (f32[112,512]{1,0:T(8,128)S(1)}, f32[112,512]{1,0:T(8,128)S(1)}, u32[]{:S(2)}, u32[]{:S(2)}) collective-permute-start(f32[112,512]{1,0:T(8,128)S(1)} %pad_maximum_fusion.28), channel_id=1, source_target_pairs={{0,2},{1,3},{2,0},{3,1},{4,6},{5,7},{6,4},{7,5},{8,10},{9,11},{10,... | collective-permute-start | bytes 688136 | tf_op jit(solution)/shard_map/ppermute | solution.py:529
  332.0 76.6 %collective-permute-start.26 = (f32[512,512]{1,0:T(8,128)S(1)}, f32[512,512]{1,0:T(8,128)S(1)}, u32[]{:S(2)}, u32[]{:S(2)}) collective-permute-start(f32[512,512]{1,0:T(8,128)S(1)} %constant_dynamic-slice_fusion.18), channel_id=1, source_target_pairs={{0,8},{4,12},{8,0},{12,4},{16,24},{20,28},{24,16},{28,20},{1,9},{5... | collective-permute-start | bytes 3145736 | tf_op jit(solution)/shard_map/ppermute | solution.py:529
  334.3 76.0 %collective-permute-start.16 = (f32[128,2048]{1,0:T(8,128)S(1)}, f32[128,2048]{1,0:T(8,128)S(1)}, u32[]{:S(2)}, u32[]{:S(2)}) collective-permute-start(f32[128,2048]{1,0:T(8,128)S(1)} %constant_dynamic-slice_fusion.23), channel_id=1, source_target_pairs={{0,16},{4,20},{8,24},{12,28},{16,0},{20,4},{24,8},{28,12},{1,17},{... | collective-permute-start | bytes 3145736 | tf_op jit(solution)/shard_map/ppermute | solution.py:529
  335.1 38.6 %collective-permute-start.37 = (f32[176,512]{1,0:T(8,128)S(1)}, f32[176,512]{1,0:T(8,128)S(1)}, u32[]{:S(2)}, u32[]{:S(2)}) collective-permute-start(f32[176,512]{1,0:T(8,128)S(1)} %constant_dynamic-slice_fusion.12), channel_id=1, source_target_pairs={{0,8},{4,12},{8,0},{12,4},{16,24},{20,28},{24,16},{28,20},{1,9},{5... | collective-permute-start | bytes 1081352 | tf_op jit(solution)/shard_map/ppermute | solution.py:529
  345.1 29.6 %collective-permute-start.57 = (f32[176,512]{1,0:T(8,128)S(1)}, f32[176,512]{1,0:T(8,128)S(1)}, u32[]{:S(2)}, u32[]{:S(2)}) collective-permute-start(f32[176,512]{1,0:T(8,128)S(1)} %constant_dynamic-slice_fusion.2), channel_id=1, source_target_pairs={{0,16},{4,20},{8,24},{12,28},{16,0},{20,4},{24,8},{28,12},{1,17},{... | collective-permute-start | bytes 1081352 | tf_op jit(solution)/shard_map/ppermute | solution.py:529
  345.5 57.1 %collective-permute-start.53 = (f32[224,512]{1,0:T(8,128)S(1)}, f32[224,512]{1,0:T(8,128)S(1)}, u32[]{:S(2)}, u32[]{:S(2)}) collective-permute-start(f32[224,512]{1,0:T(8,128)S(1)} %pad_maximum_fusion.23), channel_id=1, source_target_pairs={{0,1},{1,0},{2,3},{3,2},{4,5},{5,4},{6,7},{7,6},{8,9},{9,8},{10,11... | collective-permute-start | bytes 1376264 | tf_op jit(solution)/shard_map/ppermute | solution.py:529
  373.8 8.2 %collective-permute-start.38 = (f32[88,512]{1,0:T(8,128)S(1)}, f32[88,512]{1,0:T(8,128)S(1)}, u32[]{:S(2)}, u32[]{:S(2)}) collective-permute-start(f32[88,512]{1,0:T(8,128)S(1)} %constant_dynamic-slice_fusion.11), channel_id=1, source_target_pairs={{0,1},{1,0},{2,3},{3,2},{4,5},{5,4},{6,7},{7,6},{8,9},{9,8},{10,11... | collective-permute-start | bytes 540680 | tf_op jit(solution)/shard_map/ppermute | solution.py:529
  374.8 9.1 %collective-permute-start.58 = (f32[88,512]{1,0:T(8,128)S(1)}, f32[88,512]{1,0:T(8,128)S(1)}, u32[]{:S(2)}, u32[]{:S(2)}) collective-permute-start(f32[88,512]{1,0:T(8,128)S(1)} %constant_dynamic-slice_fusion.1), channel_id=1, source_target_pairs={{0,1},{1,0},{2,3},{3,2},{4,5},{5,4},{6,7},{7,6},{8,9},{9,8},{10,11... | collective-permute-start | bytes 540680 | tf_op jit(solution)/shard_map/ppermute | solution.py:529
  382.0 10.0 %collective-permute-start.39 = (f32[44,512]{1,0:T(8,128)S(1)}, f32[44,512]{1,0:T(8,128)S(1)}, u32[]{:S(2)}, u32[]{:S(2)}) collective-permute-start(f32[44,512]{1,0:T(8,128)S(1)} %constant_dynamic-slice_fusion.10), channel_id=1, source_target_pairs={{0,2},{1,3},{2,0},{3,1},{4,6},{5,7},{6,4},{7,5},{8,10},{9,11},{10,... | collective-permute-start | bytes 270344 | tf_op jit(solution)/shard_map/ppermute | solution.py:529
  383.9 10.2 %collective-permute-start.59 = (f32[44,512]{1,0:T(8,128)S(1)}, f32[44,512]{1,0:T(8,128)S(1)}, u32[]{:S(2)}, u32[]{:S(2)}) collective-permute-start(f32[44,512]{1,0:T(8,128)S(1)} %constant_dynamic-slice_fusion), channel_id=1, source_target_pairs={{0,2},{1,3},{2,0},{3,1},{4,6},{5,7},{6,4},{7,5},{8,10},{9,11},{10,... | collective-permute-start | bytes 270344 | tf_op jit(solution)/shard_map/ppermute | solution.py:529
  392.0 7.4 %collective-permute-start.40 = (f32[44,512]{1,0:T(8,128)S(1)}, f32[44,512]{1,0:T(8,128)S(1)}, u32[]{:S(2)}, u32[]{:S(2)}) collective-permute-start(f32[44,512]{1,0:T(8,128)S(1)} %dynamic-slice_add_fusion.23), channel_id=1, source_target_pairs={{0,2},{1,3},{2,0},{3,1},{4,6},{5,7},{6,4},{7,5},{8,10},{9,11},{10,... | collective-permute-start | bytes 270344 | tf_op jit(solution)/shard_map/ppermute | solution.py:529
  394.1 6.8 %collective-permute-start.60 = (f32[44,512]{1,0:T(8,128)S(1)}, f32[44,512]{1,0:T(8,128)S(1)}, u32[]{:S(2)}, u32[]{:S(2)}) collective-permute-start(f32[44,512]{1,0:T(8,128)S(1)} %dynamic-slice_add_fusion.22), channel_id=1, source_target_pairs={{0,2},{1,3},{2,0},{3,1},{4,6},{5,7},{6,4},{7,5},{8,10},{9,11},{10,... | collective-permute-start | bytes 270344 | tf_op jit(solution)/shard_map/ppermute | solution.py:529
  399.5 5.6 %collective-permute-start.41 = (f32[88,512]{1,0:T(8,128)S(1)}, f32[88,512]{1,0:T(8,128)S(1)}, u32[]{:S(2)}, u32[]{:S(2)}) collective-permute-start(f32[88,512]{1,0:T(8,128)S(1)} %pad_maximum_fusion.29), channel_id=1, source_target_pairs={{0,1},{1,0},{2,3},{3,2},{4,5},{5,4},{6,7},{7,6},{8,9},{9,8},{10,11... | collective-permute-start | bytes 540680 | tf_op jit(solution)/shard_map/ppermute | solution.py:529
  401.0 5.9 %collective-permute-start.61 = (f32[88,512]{1,0:T(8,128)S(1)}, f32[88,512]{1,0:T(8,128)S(1)}, u32[]{:S(2)}, u32[]{:S(2)}) collective-permute-start(f32[88,512]{1,0:T(8,128)S(1)} %pad_maximum_fusion.30), channel_id=1, source_target_pairs={{0,1},{1,0},{2,3},{3,2},{4,5},{5,4},{6,7},{7,6},{8,9},{9,8},{10,11... | collective-permute-start | bytes 540680 | tf_op jit(solution)/shard_map/ppermute | solution.py:529
  402.8 19.0 %collective-permute-start.54 = (f32[448,512]{1,0:T(8,128)S(1)}, f32[448,512]{1,0:T(8,128)S(1)}, u32[]{:S(2)}, u32[]{:S(2)}) collective-permute-start(f32[448,512]{1,0:T(8,128)S(1)} %pad_maximum_fusion.18), channel_id=1, source_target_pairs={{0,4},{4,0},{8,12},{12,8},{16,20},{20,16},{24,28},{28,24},{1,5},{5... | collective-permute-start | bytes 2752520 | tf_op jit(solution)/shard_map/ppermute | solution.py:529
  407.1 11.4 %collective-permute-start.62 = (f32[176,512]{1,0:T(8,128)S(1)}, f32[176,512]{1,0:T(8,128)S(1)}, u32[]{:S(2)}, u32[]{:S(2)}) collective-permute-start(f32[176,512]{1,0:T(8,128)S(1)} %pad_maximum_fusion.25), channel_id=1, source_target_pairs={{0,16},{4,20},{8,24},{12,28},{16,0},{20,4},{24,8},{28,12},{1,17},{... | collective-permute-start | bytes 1081352 | tf_op jit(solution)/shard_map/ppermute | solution.py:529
  408.5 11.6 %collective-permute-start.42 = (f32[176,512]{1,0:T(8,128)S(1)}, f32[176,512]{1,0:T(8,128)S(1)}, u32[]{:S(2)}, u32[]{:S(2)}) collective-permute-start(f32[176,512]{1,0:T(8,128)S(1)} %pad_maximum_fusion.24), channel_id=1, source_target_pairs={{0,8},{4,12},{8,0},{12,4},{16,24},{20,28},{24,16},{28,20},{1,9},{5... | collective-permute-start | bytes 1081352 | tf_op jit(solution)/shard_map/ppermute | solution.py:529
  408.9 20.8 %collective-permute-start.27 = (f32[256,512]{1,0:T(8,128)S(1)}, f32[256,512]{1,0:T(8,128)S(1)}, u32[]{:S(2)}, u32[]{:S(2)}) collective-permute-start(f32[256,512]{1,0:T(8,128)S(1)} %constant_dynamic-slice_fusion.17), channel_id=1, source_target_pairs={{0,16},{4,20},{8,24},{12,28},{16,0},{20,4},{24,8},{28,12},{1,17},{... | collective-permute-start | bytes 1572872 | tf_op jit(solution)/shard_map/ppermute | solution.py:529
  410.5 20.7 %collective-permute-start.17 = (f32[64,2048]{1,0:T(8,128)S(1)}, f32[64,2048]{1,0:T(8,128)S(1)}, u32[]{:S(2)}, u32[]{:S(2)}) collective-permute-start(f32[64,2048]{1,0:T(8,128)S(1)} %constant_dynamic-slice_fusion.22), channel_id=1, source_target_pairs={{0,8},{4,12},{8,0},{12,4},{16,24},{20,28},{24,16},{28,20},{1,9},{5... | collective-permute-start | bytes 1572872 | tf_op jit(solution)/shard_map/ppermute | solution.py:529
  419.5 64.1 %collective-permute-start.63 = (f32[352,512]{1,0:T(8,128)}, f32[352,512]{1,0:T(8,128)}, u32[]{:S(2)}, u32[]{:S(2)}) collective-permute-start(f32[352,512]{1,0:T(8,128)} %pad_maximum_fusion.20), channel_id=1, source_target_pairs={{0,8},{4,12},{8,0},{12,4},{16,24},{20,28},{24,16},{28,20},{1,9},{5... | collective-permute-start | bytes 2162696 | tf_op jit(solution)/shard_map/ppermute | solution.py:529
  421.1 63.9 %collective-permute-start.43 = (f32[352,512]{1,0:T(8,128)}, f32[352,512]{1,0:T(8,128)}, u32[]{:S(2)}, u32[]{:S(2)}) collective-permute-start(f32[352,512]{1,0:T(8,128)} %pad_maximum_fusion.19), channel_id=1, source_target_pairs={{0,16},{4,20},{8,24},{12,28},{16,0},{20,4},{24,8},{28,12},{1,17},{... | collective-permute-start | bytes 2162696 | tf_op jit(solution)/shard_map/ppermute | solution.py:529
  429.9 8.5 %collective-permute-start.28 = (f32[128,512]{1,0:T(8,128)S(1)}, f32[128,512]{1,0:T(8,128)S(1)}, u32[]{:S(2)}, u32[]{:S(2)}) collective-permute-start(f32[128,512]{1,0:T(8,128)S(1)} %constant_dynamic-slice_fusion.16), channel_id=1, source_target_pairs={{0,1},{1,0},{2,3},{3,2},{4,5},{5,4},{6,7},{7,6},{8,9},{9,8},{10,11... | collective-permute-start | bytes 786440 | tf_op jit(solution)/shard_map/ppermute | solution.py:529
  431.3 14.0 %collective-permute-start.18 = (f32[32,2048]{1,0:T(8,128)S(1)}, f32[32,2048]{1,0:T(8,128)S(1)}, u32[]{:S(2)}, u32[]{:S(2)}) collective-permute-start(f32[32,2048]{1,0:T(8,128)S(1)} %constant_dynamic-slice_fusion.21), channel_id=1, source_target_pairs={{0,1},{1,0},{2,3},{3,2},{4,5},{5,4},{6,7},{7,6},{8,9},{9,8},{10,11... | collective-permute-start | bytes 786440 | tf_op jit(solution)/shard_map/ppermute | solution.py:529
  438.4 8.0 %collective-permute-start.29 = (f32[64,512]{1,0:T(8,128)S(1)}, f32[64,512]{1,0:T(8,128)S(1)}, u32[]{:S(2)}, u32[]{:S(2)}) collective-permute-start(f32[64,512]{1,0:T(8,128)S(1)} %constant_dynamic-slice_fusion.15), channel_id=1, source_target_pairs={{0,2},{1,3},{2,0},{3,1},{4,6},{5,7},{6,4},{7,5},{8,10},{9,11},{10,... | collective-permute-start | bytes 393224 | tf_op jit(solution)/shard_map/ppermute | solution.py:529
  445.4 7.3 %collective-permute-start.19 = (f32[16,2048]{1,0:T(8,128)S(1)}, f32[16,2048]{1,0:T(8,128)S(1)}, u32[]{:S(2)}, u32[]{:S(2)}) collective-permute-start(f32[16,2048]{1,0:T(8,128)S(1)} %constant_dynamic-slice_fusion.20), channel_id=1, source_target_pairs={{0,2},{1,3},{2,0},{3,1},{4,6},{5,7},{6,4},{7,5},{8,10},{9,11},{10,... | collective-permute-start | bytes 393224 | tf_op jit(solution)/shard_map/ppermute | solution.py:529
  446.5 9.0 %collective-permute-start.30 = (f32[64,512]{1,0:T(8,128)S(1)}, f32[64,512]{1,0:T(8,128)S(1)}, u32[]{:S(2)}, u32[]{:S(2)}) collective-permute-start(f32[64,512]{1,0:T(8,128)S(1)} %dynamic-slice_add_fusion.19), channel_id=1, source_target_pairs={{0,2},{1,3},{2,0},{3,1},{4,6},{5,7},{6,4},{7,5},{8,10},{9,11},{10,... | collective-permute-start | bytes 393224 | tf_op jit(solution)/shard_map/ppermute | solution.py:529
  452.7 7.4 %collective-permute-start.20 = (f32[16,2048]{1,0:T(8,128)S(1)}, f32[16,2048]{1,0:T(8,128)S(1)}, u32[]{:S(2)}, u32[]{:S(2)}) collective-permute-start(f32[16,2048]{1,0:T(8,128)S(1)} %dynamic-slice_add_fusion.20), channel_id=1, source_target_pairs={{0,2},{1,3},{2,0},{3,1},{4,6},{5,7},{6,4},{7,5},{8,10},{9,11},{10,... | collective-permute-start | bytes 393224 | tf_op jit(solution)/shard_map/ppermute | solution.py:529
  455.6 6.8 %collective-permute-start.31 = (f32[128,512]{1,0:T(8,128)S(1)}, f32[128,512]{1,0:T(8,128)S(1)}, u32[]{:S(2)}, u32[]{:S(2)}) collective-permute-start(f32[128,512]{1,0:T(8,128)S(1)} %pad_maximum_fusion.27), channel_id=1, source_target_pairs={{0,1},{1,0},{2,3},{3,2},{4,5},{5,4},{6,7},{7,6},{8,9},{9,8},{10,11... | collective-permute-start | bytes 786440 | tf_op jit(solution)/shard_map/ppermute | solution.py:529
  460.2 6.4 %collective-permute-start.21 = (f32[32,2048]{1,0:T(8,128)S(1)}, f32[32,2048]{1,0:T(8,128)S(1)}, u32[]{:S(2)}, u32[]{:S(2)}) collective-permute-start(f32[32,2048]{1,0:T(8,128)S(1)} %pad_maximum_fusion.26), channel_id=1, source_target_pairs={{0,1},{1,0},{2,3},{3,2},{4,5},{5,4},{6,7},{7,6},{8,9},{9,8},{10,11... | collective-permute-start | bytes 786440 | tf_op jit(solution)/shard_map/ppermute | solution.py:529
  464.0 15.2 %collective-permute-start.32 = (f32[256,512]{1,0:T(8,128)}, f32[256,512]{1,0:T(8,128)}, u32[]{:S(2)}, u32[]{:S(2)}) collective-permute-start(f32[256,512]{1,0:T(8,128)} %pad_maximum_fusion.22), channel_id=1, source_target_pairs={{0,16},{4,20},{8,24},{12,28},{16,0},{20,4},{24,8},{28,12},{1,17},{... | collective-permute-start | bytes 1572872 | tf_op jit(solution)/shard_map/ppermute | solution.py:529
  468.2 13.4 %collective-permute-start.22 = (f32[64,2048]{1,0:T(8,128)}, f32[64,2048]{1,0:T(8,128)}, u32[]{:S(2)}, u32[]{:S(2)}) collective-permute-start(f32[64,2048]{1,0:T(8,128)} %pad_maximum_fusion.21), channel_id=1, source_target_pairs={{0,8},{4,12},{8,0},{12,4},{16,24},{20,28},{24,16},{28,20},{1,9},{5... | collective-permute-start | bytes 1572872 | tf_op jit(solution)/shard_map/ppermute | solution.py:529
  480.4 14.9 %collective-permute-start.33 = (f32[512,512]{1,0:T(8,128)S(1)}, f32[512,512]{1,0:T(8,128)S(1)}, u32[]{:S(2)}, u32[]{:S(2)}) collective-permute-start(f32[512,512]{1,0:T(8,128)S(1)} %pad_maximum_fusion.17), channel_id=1, source_target_pairs={{0,8},{4,12},{8,0},{12,4},{16,24},{20,28},{24,16},{28,20},{1,9},{5... | collective-permute-start | bytes 3145736 | tf_op jit(solution)/shard_map/ppermute | solution.py:529
  482.9 14.9 %collective-permute-start.23 = (f32[128,2048]{1,0:T(8,128)S(1)}, f32[128,2048]{1,0:T(8,128)S(1)}, u32[]{:S(2)}, u32[]{:S(2)}) collective-permute-start(f32[128,2048]{1,0:T(8,128)S(1)} %pad_maximum_fusion.16), channel_id=1, source_target_pairs={{0,16},{4,20},{8,24},{12,28},{16,0},{20,4},{24,8},{28,12},{1,17},{... | collective-permute-start | bytes 3145736 | tf_op jit(solution)/shard_map/ppermute | solution.py:529
  485.0 14.2 %collective-permute-start.64 = (f32[704,512]{1,0:T(8,128)S(1)}, f32[704,512]{1,0:T(8,128)S(1)}, u32[]{:S(2)}, u32[]{:S(2)}) collective-permute-start(f32[704,512]{1,0:T(8,128)S(1)} %pad_maximum_fusion.11), channel_id=1, source_target_pairs={{0,4},{4,0},{8,12},{12,8},{16,20},{20,16},{24,28},{28,24},{1,5},{5... | collective-permute-start | bytes 4325384 | tf_op jit(solution)/shard_map/ppermute | solution.py:529
  486.5 14.6 %collective-permute-start.44 = (f32[704,512]{1,0:T(8,128)S(1)}, f32[704,512]{1,0:T(8,128)S(1)}, u32[]{:S(2)}, u32[]{:S(2)}) collective-permute-start(f32[704,512]{1,0:T(8,128)S(1)} %pad_maximum_fusion.10), channel_id=1, source_target_pairs={{0,4},{4,0},{8,12},{12,8},{16,20},{20,16},{24,28},{28,24},{1,5},{5... | collective-permute-start | bytes 4325384 | tf_op jit(solution)/shard_map/ppermute | solution.py:529
  496.0 8.0 %collective-permute-start.34 = (f32[1024,512]{1,0:T(8,128)S(1)}, f32[1024,512]{1,0:T(8,128)S(1)}, u32[]{:S(2)}, u32[]{:S(2)}) collective-permute-start(f32[1024,512]{1,0:T(8,128)S(1)} %pad_maximum_fusion.9), channel_id=1, source_target_pairs={{0,4},{4,0},{8,12},{12,8},{16,20},{20,16},{24,28},{28,24},{1,5},{5... | collective-permute-start | bytes 6291464 | tf_op jit(solution)/shard_map/ppermute | solution.py:529
  498.2 8.7 %collective-permute-start.24 = (f32[256,2048]{1,0:T(8,128)S(1)}, f32[256,2048]{1,0:T(8,128)S(1)}, u32[]{:S(2)}, u32[]{:S(2)}) collective-permute-start(f32[256,2048]{1,0:T(8,128)S(1)} %pad_maximum_fusion.8), channel_id=1, source_target_pairs={{0,4},{4,0},{8,12},{12,8},{16,20},{20,16},{24,28},{28,24},{1,5},{5... | collective-permute-start | bytes 6291464 | tf_op jit(solution)/shard_map/ppermute | solution.py:529
  (22 other events, 120.3 us)
Sparse Core Ops, SparseCore 0:
  144.9 188.1 all-reduce.3
